TPU v7x, 32 devices: a whole 2x2x4 slice. The times are simulated.
32 devices in a mesh: rep: 2 (over y), dp: 4 (over x, core), tensor: 4 (over z).
Axes of the slice: x: 2, y: 2, z: 4, core: 2. Of those that a mesh axis runs over, the one named last changes fastest.
Arguments:
- attention: bfloat16 [3, 2048, 8192], P(None, ('rep', 'dp'), 'tensor'), parts along dimension 1, may hold values from -6 to 6
- residual: bfloat16 [3, 2048, 8192], P(None, ('rep', 'dp'), 'tensor'), parts along dimension 1, may hold values from -6 to 6
- output_weight: bfloat16 [8192, 8192], P('tensor'), may hold values from -0.09375 to 0.09375
- adapter_down_maps: bfloat16 [1024, 16, 8192], P('dp', None, 'tensor'), may hold values from -0.0625 to 0.0625
- adapter_up_maps: bfloat16 [1024, 16, 8192], P('dp', None, 'tensor'), may hold values from -1.5 to 1.5
- lacking_adapter_lists: int32 [3, 8, 4, 16], P(None, ('rep', 'dp')), parts along dimension 1, may hold values from 0 to 255
- request_slot_index: int32 [3, 2048], P(None, ('rep', 'dp')), parts along dimension 1, may hold values from 0 to 63
Outputs:
- mixed: bfloat16 [3, 2048, 8192], P(None, ('rep', 'dp'), 'tensor'), parts along dimension 1
There are 2 independent parts, one for each index of `rep`. A program takes and returns all parts, laid end to end along the dimension named above; an argument that names none is the same for every part. Nothing has to cross between parts.
All inputs are finite; a program needn't handle non-finite values.
Results may differ from a plain program's by a relative error of at most 0.011.
Values may be sent and summed in bfloat16 or wider, within the bound.
A program may use at most 256 MiB of HBM per device.

v0:
```python
import jax
import jax.numpy as jnp
from jax import lax
from jax.sharding import PartitionSpec as P

adapter_scale = 2.0


def shards(
    attention,
    residual,
    output_weight,
    adapter_down_maps,
    adapter_up_maps,
    lacking_adapter_lists,
    request_slot_index,
):
    step_count, row_count, feature_count = attention.shape
    adapter_rank_count = adapter_down_maps.shape[1]
    requested = lacking_adapter_lists[:, 0]
    owner_count = requested.shape[1]
    per_owner = requested.shape[2]
    slot_count = owner_count * per_owner
    outputs = []
    for step_index in range(step_count):
        wanted_adapter_lists = lax.all_to_all(
            requested[step_index : step_index + 1], "dp", split_axis=1, concat_axis=1, tiled=True
        )
        chosen_down_maps = jnp.take(adapter_down_maps, wanted_adapter_lists, axis=0)
        chosen_up_maps = jnp.take(adapter_up_maps, wanted_adapter_lists, axis=0)
        down_now = lax.all_to_all(chosen_down_maps, "dp", split_axis=1, concat_axis=1, tiled=True)
        up_now = lax.all_to_all(chosen_up_maps, "dp", split_axis=1, concat_axis=1, tiled=True)
        down_now = down_now[0]
        up_now = up_now[0]
        down_flat = down_now.reshape(slot_count * adapter_rank_count, feature_count)
        flattened_up_maps = up_now.reshape(slot_count * adapter_rank_count, feature_count)
        inputs = attention[step_index]
        shrink_all = lax.dot_general(
            inputs, down_flat, (((1,), (1,)), ((), ())), preferred_element_type=jnp.float32
        )
        onehot = (
            request_slot_index[step_index][:, None]
            == jnp.arange(slot_count, dtype=jnp.int32)[None, :]
        )
        picked = jnp.sum(
            jnp.where(
                onehot[:, :, None],
                shrink_all.reshape(row_count, slot_count, adapter_rank_count),
                0.0,
            ),
            axis=1,
        )
        base_term = jnp.dot(inputs, output_weight, preferred_element_type=jnp.float32)
        shrink_total = lax.psum(picked.astype(jnp.bfloat16), "tensor")
        projected_output = lax.psum_scatter(
            base_term.astype(jnp.bfloat16), "tensor", scatter_dimension=1, tiled=True
        ).astype(jnp.float32)
        expanded_width = jnp.where(
            onehot[:, :, None], shrink_total[:, None, :], jnp.zeros((), jnp.bfloat16)
        )
        expanded_width = expanded_width.reshape(row_count, slot_count * adapter_rank_count)
        adapter_output = jnp.dot(
            expanded_width, flattened_up_maps, preferred_element_type=jnp.float32
        )
        mixed = (
            residual[step_index].astype(jnp.float32)
            + projected_output
            + adapter_scale * adapter_output
        )
        outputs.append(mixed.astype(jnp.bfloat16))
    return jnp.stack(outputs)


def solution(mesh):
    placed = (
        P(None, ("rep", "dp"), "tensor"),
        P(None, ("rep", "dp"), "tensor"),
        P("tensor", None),
        P("dp", None, "tensor"),
        P("dp", None, "tensor"),
        P(None, ("rep", "dp"), None, None),
        P(None, ("rep", "dp")),
    )
    return jax.shard_map(
        shards,
        mesh=mesh,
        in_specs=placed,
        out_specs=P(None, ("rep", "dp"), "tensor"),
        check_vma=False,
    )
```

profile of v0, /device:TPU:16, one launch (start us, length us, event | category | flops | bytes accessed | tf_op | source)
XLA Modules:
  0.0 395.9 jit_solution(2288119758206445726)
XLA Ops:
  6.5 16.7 %convolution_convert_fusion.2 = bf16[256,8192]{1,0:T(8,128)(2,1)} fusion(bf16[2048,8192]{1,0:T(8,128)(2,1)} %param.11, bf16[3,256,2048]{2,1,0:T(8,128)(2,1)} %param.9), kind=kOutput, calls=%fused_computation.8 | convolution fusion | flops 8592031744 | bytes 38797312 | tf_op jit(solution)/shard_map/dot_general | solution.py:53
  24.5 6.3 %all_to_all.45 = s32[1,4,16]{2,0,1:T(1,128)S(1)} all-to-all(s32[1,4,16]{2,0,1:T(1,128)S(1)} %bitcast.101), channel_id=1, replica_groups=mesh['rep'=2,'dp'=4,'tensor'=4] {'dp'}, dimensions={1} | all-to-all | bytes 512 | tf_op jit(solution)/shard_map/all_to_all | solution.py:26
  30.8 6.1 %all_to_all.46 = s32[1,4,16]{2,0,1:T(1,128)S(1)} all-to-all(s32[1,4,16]{2,0,1:T(1,128)S(1)} %bitcast.100), channel_id=1, replica_groups=mesh['rep'=2,'dp'=4,'tensor'=4] {'dp'}, dimensions={1} | all-to-all | bytes 512 | tf_op jit(solution)/shard_map/all_to_all | solution.py:26
  40.3 8.6 %gather_fusion.2 = bf16[64,16,2048]{2,1,0:T(8,128)(2,1)} fusion(bf16[256,16,2048]{2,1,0:T(8,128)(2,1)} %param.12, s32[1024]{0:T(1024)S(1)} %pad_clamp_fusion.1), kind=kCustom, calls=%fused_computation.2.clone | custom fusion | bytes 8388864 | tf_op jit(solution)/shard_map/jit(_take)/gather | solution.py:29
  48.8 8.6 %gather_fusion.3 = bf16[64,16,2048]{2,1,0:T(8,128)(2,1)} fusion(bf16[256,16,2048]{2,1,0:T(8,128)(2,1)} %param.13, s32[1024]{0:T(1024)S(1)} %pad_clamp_fusion.1), kind=kCustom, calls=%fused_computation.3.clone | custom fusion | bytes 8388864 | tf_op jit(solution)/shard_map/jit(_take)/gather | solution.py:30
  57.5 6.0 %broadcast_select_fusion.2 = (bf16[1,4,16,16,2048]{4,3,2,0,1:T(8,128)(2,1)}, bf16[1,4,16,16,2048]{4,3,2,0,1:T(8,128)(2,1)}) fusion(bf16[1,4,16,16,2048]{4,3,2,0,1:T(8,128)(2,1)} %bitcast.88, pred[4,16]{1,0:T(4,128)(4,1)S(1)} %bitcast.105, bf16[1,4,16,16,2048]{4,3,2,0,1:T(8,128)(2,1)} %bitcast.87), kind=kLoop, calls=%fused_computation.11 | loop fusion | flops 4194304 | bytes 16777280 | tf_op jit(solution)/shard_map/jit(_take)/select_n | solution.py:30
  63.4 4.9 %all-to-all-start.4 = ((bf16[1,4,16,16,2048]{4,3,2,0,1:T(8,128)(2,1)}), bf16[1,4,16,16,2048]{4,3,2,0,1:T(8,128)(2,1)}, u32[]{:S(2)}, u32[]{:S(2)}) async-start(bf16[1,4,16,16,2048]{4,3,2,0,1:T(8,128)(2,1)} %get-tuple-element.18), calls=%async_computation.6 | async-start | bytes 8388608 | tf_op jit(solution)/shard_map/all_to_all | solution.py:31
  68.5 8.6 %gather_fusion.1 = bf16[64,16,2048]{2,1,0:T(8,128)(2,1)} fusion(bf16[256,16,2048]{2,1,0:T(8,128)(2,1)} %param.13, s32[1024]{0:T(1024)S(1)} %pad_clamp_fusion.2), kind=kCustom, calls=%fused_computation.1.clone | custom fusion | bytes 8388864 | tf_op jit(solution)/shard_map/jit(_take)/gather | solution.py:30
  77.1 8.5 %gather_fusion = bf16[64,16,2048]{2,1,0:T(8,128)(2,1)} fusion(bf16[256,16,2048]{2,1,0:T(8,128)(2,1)} %param.12, s32[1024]{0:T(1024)S(1)} %pad_clamp_fusion.2), kind=kCustom, calls=%fused_computation.clone | custom fusion | bytes 8388864 | tf_op jit(solution)/shard_map/jit(_take)/gather | solution.py:29
  85.6 6.0 %broadcast_select_fusion.4 = (bf16[1,4,16,16,2048]{4,3,2,0,1:T(8,128)(2,1)}, bf16[1,4,16,16,2048]{4,3,2,0,1:T(8,128)(2,1)}) fusion(bf16[1,4,16,16,2048]{4,3,2,0,1:T(8,128)(2,1)} %bitcast.89, pred[4,16]{1,0:T(4,128)(4,1)S(1)} %bitcast.106, bf16[1,4,16,16,2048]{4,3,2,0,1:T(8,128)(2,1)} %bitcast.90), kind=kLoop, calls=%fused_computation.13 | loop fusion | flops 4194304 | bytes 16777280 | tf_op jit(solution)/shard_map/jit(_take)/select_n | solution.py:30
  91.6 25.0 %all-to-all-done.4 = bf16[1,4,16,16,2048]{4,3,2,0,1:T(8,128)(2,1)} async-done(((bf16[1,4,16,16,2048]{4,3,2,0,1:T(8,128)(2,1)}), bf16[1,4,16,16,2048]{4,3,2,0,1:T(8,128)(2,1)}, u32[]{:S(2)}, u32[]{:S(2)}) %all-to-all-start.4) | async-done | bytes 4194336 | tf_op jit(solution)/shard_map/all_to_all | solution.py:31
  116.6 5.1 %all-to-all-start.1 = ((bf16[1,4,16,16,2048]{4,3,2,0,1:T(8,128)(2,1)}), bf16[1,4,16,16,2048]{4,3,2,0,1:T(8,128)(2,1)}, u32[]{:S(2)}, u32[]{:S(2)}) async-start(bf16[1,4,16,16,2048]{4,3,2,0,1:T(8,128)(2,1)} %get-tuple-element.16), calls=%async_computation.2 | async-start | bytes 8388608 | tf_op jit(solution)/shard_map/all_to_all | solution.py:31
  121.8 16.4 %convolution_convert_fusion.1 = bf16[256,8192]{1,0:T(8,128)(2,1)} fusion(bf16[2048,8192]{1,0:T(8,128)(2,1)} %param.11, bf16[3,256,2048]{2,1,0:T(8,128)(2,1)S(1)} %copy-done.3), kind=kOutput, calls=%fused_computation.7 | convolution fusion | flops 8592031744 | bytes 38797312 | tf_op jit(solution)/shard_map/dot_general | solution.py:53
  138.3 8.8 %gather_fusion.4 = bf16[64,16,2048]{2,1,0:T(8,128)(2,1)} fusion(bf16[256,16,2048]{2,1,0:T(8,128)(2,1)} %param.12, s32[1024]{0:T(1024)S(1)} %pad_clamp_fusion), kind=kCustom, calls=%fused_computation.4.clone | custom fusion | bytes 8388864 | tf_op jit(solution)/shard_map/jit(_take)/gather | solution.py:29
  147.1 8.6 %gather_fusion.5 = bf16[64,16,2048]{2,1,0:T(8,128)(2,1)} fusion(bf16[256,16,2048]{2,1,0:T(8,128)(2,1)} %param.13, s32[1024]{0:T(1024)S(1)} %pad_clamp_fusion), kind=kCustom, calls=%fused_computation.5.clone | custom fusion | bytes 8388864 | tf_op jit(solution)/shard_map/jit(_take)/gather | solution.py:30
  155.6 6.0 %broadcast_select_fusion = (bf16[1,4,16,16,2048]{4,3,2,0,1:T(8,128)(2,1)}, bf16[1,4,16,16,2048]{4,3,2,0,1:T(8,128)(2,1)}) fusion(bf16[1,4,16,16,2048]{4,3,2,0,1:T(8,128)(2,1)} %bitcast.92, pred[4,16]{1,0:T(4,128)(4,1)S(1)} %bitcast.107, bf16[1,4,16,16,2048]{4,3,2,0,1:T(8,128)(2,1)} %bitcast.91), kind=kLoop, calls=%fused_computation.9 | loop fusion | flops 4194304 | bytes 16777280 | tf_op jit(solution)/shard_map/jit(_take)/select_n | solution.py:30
  161.7 8.2 %all-to-all-done.1 = bf16[1,4,16,16,2048]{4,3,2,0,1:T(8,128)(2,1)} async-done(((bf16[1,4,16,16,2048]{4,3,2,0,1:T(8,128)(2,1)}), bf16[1,4,16,16,2048]{4,3,2,0,1:T(8,128)(2,1)}, u32[]{:S(2)}, u32[]{:S(2)}) %all-to-all-start.1) | async-done | bytes 4194336 | tf_op jit(solution)/shard_map/all_to_all | solution.py:31
  169.9 53.9 %all_to_all.47 = bf16[1,4,16,16,2048]{4,3,2,0,1:T(8,128)(2,1)} all-to-all(bf16[1,4,16,16,2048]{4,3,2,0,1:T(8,128)(2,1)} %get-tuple-element.20), channel_id=1, replica_groups=mesh['rep'=2,'dp'=4,'tensor'=4] {'dp'}, dimensions={1} | all-to-all | bytes 8388608 | tf_op jit(solution)/shard_map/all_to_all | solution.py:31
  228.9 16.4 %convolution_convert_fusion = bf16[256,8192]{1,0:T(8,128)(2,1)} fusion(bf16[2048,8192]{1,0:T(8,128)(2,1)} %param.11, bf16[3,256,2048]{2,1,0:T(8,128)(2,1)S(1)} %copy-done.3), kind=kOutput, calls=%fused_computation.6 | convolution fusion | flops 8592031744 | bytes 38797312 | tf_op jit(solution)/shard_map/dot_general | solution.py:53
  245.3 31.6 %all-to-all-done.2 = bf16[1,4,16,16,2048]{4,3,2,0,1:T(8,128)(2,1)} async-done(((bf16[1,4,16,16,2048]{4,3,2,0,1:T(8,128)(2,1)}), bf16[1,4,16,16,2048]{4,3,2,0,1:T(8,128)(2,1)}, u32[]{:S(2)}, u32[]{:S(2)}) %all-to-all-start.2) | async-done | bytes 4194336 | tf_op jit(solution)/shard_map/all_to_all | solution.py:32
  276.9 5.0 %all-to-all-start.5 = ((bf16[1,4,16,16,2048]{4,3,2,0,1:T(8,128)(2,1)}), bf16[1,4,16,16,2048]{4,3,2,0,1:T(8,128)(2,1)}, u32[]{:S(2)}, u32[]{:S(2)}) async-start(bf16[1,4,16,16,2048]{4,3,2,0,1:T(8,128)(2,1)} %get-tuple-element.17), calls=%async_computation.7 | async-start | bytes 8388608 | tf_op jit(solution)/shard_map/all_to_all | solution.py:32
  282.0 48.1 %all-to-all-done.5 = bf16[1,4,16,16,2048]{4,3,2,0,1:T(8,128)(2,1)} async-done(((bf16[1,4,16,16,2048]{4,3,2,0,1:T(8,128)(2,1)}), bf16[1,4,16,16,2048]{4,3,2,0,1:T(8,128)(2,1)}, u32[]{:S(2)}, u32[]{:S(2)}) %all-to-all-start.5) | async-done | bytes 4194336 | tf_op jit(solution)/shard_map/all_to_all | solution.py:32
  344.6 17.3 %all-reduce = (bf16[256,16]{0,1:T(8,128)(2,1)S(1)}, bf16[256,16]{0,1:T(8,128)(2,1)S(1)}, bf16[256,16]{0,1:T(8,128)(2,1)S(1)}) all-reduce(bf16[256,16]{0,1:T(8,128)(2,1)S(1)} %select_reduce_fusion, bf16[256,16]{0,1:T(8,128)(2,1)S(1)} %select_reduce_fusion.1, ...), channel_id=1, replica_groups=mesh['rep'=2,'dp'=4,'tensor'=4] {'tensor'}, use_global_device_ids=true, to_apply=%region_8.10 | all-reduce | flops 12288 | bytes 49152 | tf_op jit(solution)/shard_map/psum | solution.py:54
  370.6 12.7 %all-to-all-done.8 = bf16[1,4,16,16,2048]{4,3,2,0,1:T(8,128)(2,1)} async-done(((bf16[1,4,16,16,2048]{4,3,2,0,1:T(8,128)(2,1)}), bf16[1,4,16,16,2048]{4,3,2,0,1:T(8,128)(2,1)}, u32[]{:S(2)}, u32[]{:S(2)}) %all-to-all-start.8) | async-done | bytes 4194336 | tf_op jit(solution)/shard_map/all_to_all | solution.py:32
  (55 shorter events, 39.2 us)
Async XLA Ops:
  6.5 355.7 %reduce-scatter.4.cloned.1.call-start = ((), (), s32[]{:S(2)}) async-start(), calls=%async_computation.12 | async-start | bytes 5242880 | tf_op jit(solution)/shard_map/reduce_scatter | solution.py:55
  23.3 0.7 copy-start.1
  36.9 26.5 %all-to-all-start.6 = ((s32[1,4,16]{2,0,1:T(1,128)}), s32[1,4,16]{2,0,1:T(1,128)S(1)}, u32[]{:S(2)}, u32[]{:S(2)}) async-start(s32[1,4,16]{2,0,1:T(1,128)} %bitcast.30), calls=%async_computation.9 | async-start | bytes 4096 | tf_op jit(solution)/shard_map/all_to_all | solution.py:26
  63.4 53.2 %all-to-all-start.4 = ((bf16[1,4,16,16,2048]{4,3,2,0,1:T(8,128)(2,1)}), bf16[1,4,16,16,2048]{4,3,2,0,1:T(8,128)(2,1)}, u32[]{:S(2)}, u32[]{:S(2)}) async-start(bf16[1,4,16,16,2048]{4,3,2,0,1:T(8,128)(2,1)} %get-tuple-element.18), calls=%async_computation.6 | async-start | bytes 8388608 | tf_op jit(solution)/shard_map/all_to_all | solution.py:31
  116.6 5.2 %copy-start.3 = (bf16[3,256,2048]{2,1,0:T(8,128)(2,1)S(1)}, bf16[3,256,2048]{2,1,0:T(8,128)(2,1)}, u32[]{:S(2)}) copy-start(bf16[3,256,2048]{2,1,0:T(8,128)(2,1)} %param.9) | copy-start | bytes 9437188
  116.6 53.3 %all-to-all-start.1 = ((bf16[1,4,16,16,2048]{4,3,2,0,1:T(8,128)(2,1)}), bf16[1,4,16,16,2048]{4,3,2,0,1:T(8,128)(2,1)}, u32[]{:S(2)}, u32[]{:S(2)}) async-start(bf16[1,4,16,16,2048]{4,3,2,0,1:T(8,128)(2,1)} %get-tuple-element.16), calls=%async_computation.2 | async-start | bytes 8388608 | tf_op jit(solution)/shard_map/all_to_all | solution.py:31
  121.7 244.7 %reduce-scatter.6.cloned.1.call-start = ((), (), s32[]{:S(2)}) async-start(), calls=%async_computation.13 | async-start | bytes 5242880 | tf_op jit(solution)/shard_map/reduce_scatter | solution.py:55
  223.8 53.1 %all-to-all-start.2 = ((bf16[1,4,16,16,2048]{4,3,2,0,1:T(8,128)(2,1)}), bf16[1,4,16,16,2048]{4,3,2,0,1:T(8,128)(2,1)}, u32[]{:S(2)}, u32[]{:S(2)}) async-start(bf16[1,4,16,16,2048]{4,3,2,0,1:T(8,128)(2,1)} %get-tuple-element.15), calls=%async_computation.3 | async-start | bytes 8388608 | tf_op jit(solution)/shard_map/all_to_all | solution.py:32
  228.7 154.6 %reduce-scatter.8.cloned.1.call-start = ((), (), s32[]{:S(2)}) async-start(), calls=%async_computation.14 | async-start | bytes 5242880 | tf_op jit(solution)/shard_map/reduce_scatter | solution.py:55
  276.9 5.1 %copy-start.2 = (s32[3,256]{1,0:T(4,128)S(1)}, s32[3,256]{1,0:T(4,128)}, u32[]{:S(2)}) copy-start(s32[3,256]{1,0:T(4,128)} %param.15) | copy-start | bytes 9220
  276.9 53.3 %all-to-all-start.5 = ((bf16[1,4,16,16,2048]{4,3,2,0,1:T(8,128)(2,1)}), bf16[1,4,16,16,2048]{4,3,2,0,1:T(8,128)(2,1)}, u32[]{:S(2)}, u32[]{:S(2)}) async-start(bf16[1,4,16,16,2048]{4,3,2,0,1:T(8,128)(2,1)} %get-tuple-element.17), calls=%async_computation.7 | async-start | bytes 8388608 | tf_op jit(solution)/shard_map/all_to_all | solution.py:32
  330.2 53.1 %all-to-all-start.8 = ((bf16[1,4,16,16,2048]{4,3,2,0,1:T(8,128)(2,1)}), bf16[1,4,16,16,2048]{4,3,2,0,1:T(8,128)(2,1)}, u32[]{:S(2)}, u32[]{:S(2)}) async-start(bf16[1,4,16,16,2048]{4,3,2,0,1:T(8,128)(2,1)} %get-tuple-element.19), calls=%async_computation.11 | async-start | bytes 8388608 | tf_op jit(solution)/shard_map/all_to_all | solution.py:32
  335.0 4.2 %copy-start.4 = (bf16[3,256,2048]{2,1,0:T(8,128)(2,1)S(1)}, bf16[3,256,2048]{2,1,0:T(8,128)(2,1)}, u32[]{:S(2)}) copy-start(bf16[3,256,2048]{2,1,0:T(8,128)(2,1)} %param.9) | copy-start | bytes 9437188
  339.2 3.9 copy-start
Sparse Core Ops, SparseCore 0:
  23.4 78.3 reduce-scatter.3
  138.3 78.8 reduce-scatter.5
  245.4 78.6 reduce-scatter.7
where the time goes:
time: 398 us; the launch traced here: 396 us
  waiting for transfers between devices  126 us (32%)
  blocking collectives  83.5 us (21%)
  matrix products  70.8 us (18%)
  local copies, waits for them, and re-layouts  53.2 us (13%)
  starting transfers between devices  28.3 us (7%)
  other arithmetic  21 us (5%)
  between operations  13.3 us (3%)
    all_to_all x3, waiting for transfers between devices, shards(): lax.all_to_all(chosen_up_maps, 'dp', split_axis=1, concat_axis=1, tiled=T...  92.4 us
    all_to_all x1, blocking collectives, shards(): lax.all_to_all(chosen_down_maps, 'dp', split_axis=1, concat_axis=1, tiled...  53.9 us
    dot_general x3, matrix products, shards(): jnp.dot(inputs, output_weight, preferred_element_type=jnp.float32)  49.5 us
    all_to_all x2, waiting for transfers between devices, shards(): lax.all_to_all(chosen_down_maps, 'dp', split_axis=1, concat_axis=1, tiled...  33.2 us
    gather x3, local copies, waits for them, and re-layouts, shards(): chosen_down_maps = jnp.take(adapter_down_maps, wanted_adapter_lists, axis=0)  25.9 us
    gather x3, local copies, waits for them, and re-layouts, shards(): chosen_up_maps = jnp.take(adapter_up_maps, wanted_adapter_lists, axis=0)  25.8 us
    select_n x3, other arithmetic, shards(): chosen_up_maps = jnp.take(adapter_up_maps, wanted_adapter_lists, axis=0)  18 us
    psum x1, blocking collectives, shards(): shrink_total = lax.psum(picked.astype(jnp.bfloat16), 'tensor')  17.3 us
  transfers between devices with their start and end apart: 9, of which 5 were waited for; matrix products, arithmetic and copies ran while one was open for 31% of the time, Pallas kernels for 0%

commit v1 on v0

v1 whole, which is shorter than its diff:
```python
import functools

import jax
import jax.numpy as jnp
from jax import lax
from jax.experimental import pallas as pl
from jax.experimental.pallas import tpu as pltpu
from jax.sharding import PartitionSpec as P

adapter_scale = 2.0
MESH = pl.DeviceIdType.MESH


def project_kernel(
    n, per_block, tile, a_ref, w_hbm, o_ref, w_buf, part, from_left, from_right,
    w_sem, left_sem, right_sem, to_right_sem, to_left_sem,
):
    me = lax.axis_index("tensor")
    steps = (n - 1) * per_block

    def fetch(t):
        return pltpu.make_async_copy(
            w_hbm.at[:, pl.ds(pl.multiple_of(t * tile, tile), tile)], w_buf.at[t], w_sem.at[t]
        )

    def send_right(t):
        return pltpu.make_async_remote_copy(
            src_ref=from_left.at[t], dst_ref=from_left.at[t],
            send_sem=to_right_sem.at[t], recv_sem=left_sem.at[t],
            device_id={"tensor": me + 1}, device_id_type=MESH,
        )

    def send_left(t):
        return pltpu.make_async_remote_copy(
            src_ref=from_right.at[t], dst_ref=from_right.at[t],
            send_sem=to_left_sem.at[t], recv_sem=right_sem.at[t],
            device_id={"tensor": me - 1}, device_id_type=MESH,
        )

    def blocks(i):
        turn, piece = i // per_block, i % per_block
        return n - 1 - turn, turn, piece

    def fetch_step(i, carry):
        right_block, left_block, piece = blocks(i)

        @pl.when(right_block > me)
        def _():
            fetch(right_block * per_block + piece).start()

        @pl.when(left_block < me)
        def _():
            fetch(left_block * per_block + piece).start()

        return carry

    def fetch_own(i, carry):
        fetch(me * per_block + i).start()
        return carry

    lax.fori_loop(0, steps, fetch_step, 0)
    lax.fori_loop(0, per_block, fetch_own, 0)

    barrier = pltpu.get_barrier_semaphore()

    @pl.when(me > 0)
    def _():
        pl.semaphore_signal(barrier, inc=1, device_id={"tensor": me - 1}, device_id_type=MESH)

    @pl.when(me < n - 1)
    def _():
        pl.semaphore_signal(barrier, inc=1, device_id={"tensor": me + 1}, device_id_type=MESH)

    peers = (me > 0).astype(jnp.int32) + (me < n - 1).astype(jnp.int32)
    pl.semaphore_wait(barrier, peers)

    def product(t):
        fetch(t).wait()
        part[...] = jnp.dot(a_ref[...], w_buf[t], preferred_element_type=jnp.float32)

    def step(i, carry):
        right_block, left_block, piece = blocks(i)

        @pl.when(right_block > me)
        def _():
            t = right_block * per_block + piece
            product(t)

            @pl.when(me > 0)
            def _():
                send_right(t).wait_recv()
                part[...] += from_left[t].astype(jnp.float32)

            from_left[t] = part[...].astype(jnp.bfloat16)
            send_right(t).start()

        @pl.when(left_block < me)
        def _():
            t = left_block * per_block + piece
            product(t)

            @pl.when(me < n - 1)
            def _():
                send_left(t).wait_recv()
                part[...] += from_right[t].astype(jnp.float32)

            from_right[t] = part[...].astype(jnp.bfloat16)
            send_left(t).start()

        return carry

    lax.fori_loop(0, steps, step, 0)

    def own(i, carry):
        t = me * per_block + i
        product(t)

        @pl.when(me > 0)
        def _():
            send_right(t).wait_recv()
            part[...] += from_left[t].astype(jnp.float32)

        @pl.when(me < n - 1)
        def _():
            send_left(t).wait_recv()
            part[...] += from_right[t].astype(jnp.float32)

        o_ref[i] = part[...]
        return carry

    lax.fori_loop(0, per_block, own, 0)

    def drain(i, carry):
        right_block, left_block, piece = blocks(i)

        @pl.when(right_block > me)
        def _():
            send_right(right_block * per_block + piece).wait_send()

        @pl.when(left_block < me)
        def _():
            send_left(left_block * per_block + piece).wait_send()

        return carry

    lax.fori_loop(0, steps, drain, 0)


def project(inputs, weight, n, collective_id):
    rows, depth = inputs.shape
    columns = weight.shape[1]
    width = columns // n
    tile = min(256, width)
    per_block = width // tile
    tiles = n * per_block
    return pl.pallas_call(
        functools.partial(project_kernel, n, per_block, tile),
        out_shape=jax.ShapeDtypeStruct((per_block, rows, tile), jnp.float32),
        in_specs=[
            pl.BlockSpec(memory_space=pltpu.VMEM),
            pl.BlockSpec(memory_space=pl.ANY),
        ],
        out_specs=pl.BlockSpec(memory_space=pltpu.VMEM),
        scratch_shapes=[
            pltpu.VMEM((tiles, depth, tile), jnp.bfloat16),
            pltpu.VMEM((rows, tile), jnp.float32),
            pltpu.VMEM((tiles, rows, tile), jnp.bfloat16),
            pltpu.VMEM((tiles, rows, tile), jnp.bfloat16),
            pltpu.SemaphoreType.DMA((tiles,)),
            pltpu.SemaphoreType.DMA((tiles,)),
            pltpu.SemaphoreType.DMA((tiles,)),
            pltpu.SemaphoreType.DMA((tiles,)),
            pltpu.SemaphoreType.DMA((tiles,)),
        ],
        compiler_params=pltpu.CompilerParams(
            collective_id=collective_id, has_side_effects=True, vmem_limit_bytes=60 * 2**20
        ),
        cost_estimate=pl.CostEstimate(
            flops=2 * rows * depth * columns,
            bytes_accessed=2 * depth * columns + 64 * rows * width,
            transcendentals=0,
        ),
    )(inputs, weight)


def shards(
    groups,
    n,
    attention,
    residual,
    output_weight,
    adapter_down_maps,
    adapter_up_maps,
    lacking_adapter_lists,
    request_slot_index,
):
    step_count, row_count, feature_count = attention.shape
    rank = adapter_down_maps.shape[1]
    width = residual.shape[2]
    owners, per_owner = lacking_adapter_lists.shape[2:]
    me = lax.axis_index("dp")

    everyone = lax.all_gather(attention, "dp", axis=0)
    small = jnp.concatenate(
        [lacking_adapter_lists[:, 0].reshape(step_count, -1), request_slot_index], axis=1
    )
    small = lax.all_gather(small, "dp", axis=0)
    wanted = small[:, :, : owners * per_owner].reshape(groups, step_count, owners, per_owner)
    wanted = lax.dynamic_index_in_dim(wanted, me, axis=2, keepdims=False)
    slots = small[:, :, owners * per_owner :] - me * per_owner
    down_now = jnp.take(adapter_down_maps, wanted, axis=0).reshape(
        groups, step_count, per_owner * rank, feature_count
    )
    up_now = jnp.take(adapter_up_maps, wanted, axis=0).reshape(
        groups, step_count, per_owner * rank, width
    )

    first = project(attention[0], output_weight, n, 1)

    mine = slots[..., None] == jnp.arange(per_owner, dtype=jnp.int32)
    everyone, first = lax.optimization_barrier((everyone, first))
    shrink_all = lax.dot_general(
        everyone, down_now, (((3,), (3,)), ((0, 1), (0, 1))), preferred_element_type=jnp.float32
    ).reshape(groups, step_count, row_count, per_owner, rank)
    picked = jnp.sum(jnp.where(mine[..., None], shrink_all, 0.0), axis=3)
    shrink = lax.psum(picked.astype(jnp.bfloat16), "tensor")
    expanded = jnp.where(mine[..., None], shrink[:, :, :, None, :], jnp.zeros((), jnp.bfloat16))
    expanded = expanded.reshape(groups, step_count, row_count, per_owner * rank)
    lora = lax.dot_general(
        expanded, up_now, (((3,), (2,)), ((0, 1), (0, 1))), preferred_element_type=jnp.float32
    ).astype(jnp.bfloat16)

    lora, rest_in = lax.optimization_barrier(
        (lora, attention[1:].reshape((step_count - 1) * row_count, feature_count))
    )
    rest = project(rest_in, output_weight, n, 2)
    lora_own = lax.psum_scatter(lora, "dp", scatter_dimension=0, tiled=False)

    def placed(pieces, steps):
        per_block, rows, tile = pieces.shape
        return pieces.transpose(1, 0, 2).reshape(steps, row_count, per_block * tile)

    projected = jnp.concatenate([placed(first, 1), placed(rest, step_count - 1)], axis=0)
    mixed = (
        residual.astype(jnp.float32)
        + projected
        + adapter_scale * lora_own.astype(jnp.float32)
    )
    return mixed.astype(jnp.bfloat16)


def solution(mesh):
    placed = (
        P(None, ("rep", "dp"), "tensor"),
        P(None, ("rep", "dp"), "tensor"),
        P("tensor", None),
        P("dp", None, "tensor"),
        P("dp", None, "tensor"),
        P(None, ("rep", "dp"), None, None),
        P(None, ("rep", "dp")),
    )
    return jax.shard_map(
        functools.partial(shards, mesh.shape["dp"], mesh.shape["tensor"]),
        mesh=mesh,
        in_specs=placed,
        out_specs=P(None, ("rep", "dp"), "tensor"),
        check_vma=False,
    )
```

time: 398 us -> 420 us (1.055)
  Pallas kernels: 0 us -> 269 us
  waiting for transfers between devices: 126 us -> 34 us
  blocking collectives: 83.5 us -> 5.18 us
  matrix products: 70.8 us -> 21.1 us
  starting transfers between devices: 28.3 us -> 0.08 us
  other arithmetic: 21 us -> 26.5 us
    pallas_call x0 -> x2, Pallas kernels: none -> 269 us  [project(): pl.pallas_call(functools.partial(project_kernel, n, per_block, tile), out...]
    all_to_all x6 -> x0, waiting for transfers between devices: 126 us -> none  [the longest x3 92.4 us: shards(): lax.all_to_all(chosen_up_maps, 'dp', split_axis=1, concat_axis=1, tiled=T...]
    all_to_all x3 -> x0, blocking collectives: 66.2 us -> none  [the longest x1 53.9 us: shards(): lax.all_to_all(chosen_down_maps, 'dp', split_axis=1, concat_axis=1, tiled...]
    dot_general x9 -> x2, matrix products: 70.8 us -> 21.1 us  [the longest x1 11.1 us: shards(): lax.dot_general(expanded, up_now, (((3,), (2,)), ((0, 1), (0, 1))), prefe...]
    psum x0 -> x1, waiting for transfers between devices: none -> 33.3 us  [shards(): shrink = lax.psum(picked.astype(jnp.bfloat16), 'tensor')]
    all_to_all x6 -> x0, starting transfers between devices: 28 us -> none  [the longest x3 14.7 us: shards(): lax.all_to_all(chosen_up_maps, 'dp', split_axis=1, concat_axis=1, tiled=T...]
    gather x6 -> x2, local copies, waits for them, and re-layouts: 51.7 us -> 30.4 us  [the longest x1 16.2 us: shards(): jnp.take(adapter_up_maps, wanted, axis=0)]
    psum x1 -> x0, blocking collectives: 17.3 us -> none  [shards(): shrink_total = lax.psum(picked.astype(jnp.bfloat16), 'tensor')]
  transfers between devices with their start and end apart: 9 -> 3, of which waited for: 5 -> 1; matrix products, arithmetic and copies ran while one was open for 31% -> 16% of each run, Pallas kernels for 0% -> 64%
where the time goes in v1:
time: 420 us
  Pallas kernels  269 us (64%)
  local copies, waits for them, and re-layouts  50.6 us (12%)
  waiting for transfers between devices  34 us (8%)
  other arithmetic  26.5 us (6%)
  matrix products  21.1 us (5%)
  between operations  13.2 us (3%)
  blocking collectives  5.18 us (1%)
    pallas_call x2, Pallas kernels, project(): pl.pallas_call(functools.partial(project_kernel, n, per_block, tile), out...  269 us
    psum x1, waiting for transfers between devices, shards(): shrink = lax.psum(picked.astype(jnp.bfloat16), 'tensor')  33.3 us
    select_n x1, other arithmetic, shards(): jnp.take(adapter_up_maps, wanted, axis=0)  17.4 us
    gather x1, local copies, waits for them, and re-layouts, shards(): jnp.take(adapter_up_maps, wanted, axis=0)  16.2 us
    gather x1, local copies, waits for them, and re-layouts, shards(): jnp.take(adapter_down_maps, wanted, axis=0)  14.2 us
    dot_general x1, matrix products, shards(): lax.dot_general(expanded, up_now, (((3,), (2,)), ((0, 1), (0, 1))), prefe...  11.1 us
    dot_general x1, matrix products, shards(): lax.dot_general(everyone, down_now, (((3,), (3,)), ((0, 1), (0, 1))), pre...  10 us
  transfers between devices with their start and end apart: 3, of which 1 were waited for; matrix products, arithmetic and copies ran while one was open for 16% of the time, Pallas kernels for 64%

profile of v1, /device:TPU:16, one launch (start us, length us, event | category | flops | bytes accessed | tf_op | source)
XLA Modules:
  0.0 419.9 jit_solution(17974927463413253075)
XLA Ops:
  6.5 0.7 all-gather.5.cloned.1.call-update
  7.3 0.8 reshape_squeeze.3
  8.1 0.8 add_bitcast_fusion
  8.8 5.2 %all-gather.2 = s32[4,3,320]{2,1,0:T(4,128)S(1)} all-gather(s32[1,3,320]{2,1,0:T(4,128)S(1)} %add_bitcast_fusion), channel_id=3, replica_groups=mesh['rep'=2,'dp'=4,'tensor'=4] {'dp'}, dimensions={0}, use_global_device_ids=true | all-gather | bytes 19200 | tf_op jit(solution)/shard_map/all_gather | solution.py:207
  14.0 0.1 reshape.40
  14.2 0.1 reshape.71
  14.3 16.2 %gather_fusion.1 = bf16[192,16,2048]{2,1,0:T(8,128)(2,1)} fusion(bf16[256,16,2048]{2,1,0:T(8,128)(2,1)} %param.13, s32[1024]{0:T(1024)S(1)} %pad_clamp_fusion), kind=kCustom, calls=%fused_computation.1.clone | custom fusion | bytes 25166592 | tf_op jit(solution)/shard_map/jit(_take)/gather | solution.py:214
  30.4 14.2 %gather_fusion = bf16[192,16,2048]{2,1,0:T(8,128)(2,1)} fusion(bf16[256,16,2048]{2,1,0:T(8,128)(2,1)} %param.12, s32[1024]{0:T(1024)S(1)} %pad_clamp_fusion), kind=kCustom, calls=%fused_computation.clone | custom fusion | bytes 25166592 | tf_op jit(solution)/shard_map/jit(_take)/gather | solution.py:211
  44.8 1.0 slice_bitcast_fusion.a_ref
  45.8 102.4 %shard_map.73 = f32[8,256,256]{2,1,0:T(8,128)} custom-call(bf16[256,2048]{1,0:T(8,128)(2,1)} %slice_bitcast_fusion.a_ref, bf16[2048,8192]{1,0:T(8,128)(2,1)} %w_hbm.3), custom_call_target="tpu_custom_call" | custom-call | flops 8589934592 | bytes 67108864 | tf_op jit(solution)/shard_map/pallas_call | solution.py:156
  148.3 17.4 %broadcast_select_fusion = (bf16[4,3,16,16,2048]{4,3,2,1,0:T(8,128)(2,1)}, bf16[4,3,16,16,2048]{4,3,2,1,0:T(8,128)(2,1)}) fusion(bf16[4,3,16,16,2048]{4,3,2,1,0:T(8,128)(2,1)} %bitcast.25, pred[4,3,16]{2,1,0:T(4,128)(4,1)S(1)} %copy.20, bf16[4,3,16,16,2048]{4,3,2,1,0:T(8,128)(2,1)} %bitcast.26), kind=kLoop, calls=%fused_computation.2 | loop fusion | flops 12582912 | bytes 50331840 | tf_op jit(solution)/shard_map/jit(_take)/select_n | solution.py:214
  165.7 10.0 %fusion.2 = f32[4,3,256,256]{2,3,1,0:T(8,128)S(1)} fusion(bf16[4,3,256,2048]{3,2,1,0:T(8,128)(2,1)} %bitcast.36, bf16[4,3,256,2048]{3,2,1,0:T(8,128)(2,1)} %bitcast.27), kind=kOutput, calls=%fused_computation.18 | convolution fusion | flops 3221225472 | bytes 28311552 | tf_op jit(solution)/shard_map/dot_general | solution.py:222
  175.7 1.1 select_reduce_fusion
  177.0 1.5 slice.15
  178.4 33.3 %all-reduce.2.cloned.1.call-done = bf16[4,3,256,16]{2,3,1,0:T(8,128)(2,1)} async-done(((bf16[4,3,256,16]{2,3,1,0:T(8,128)(2,1)}), bf16[4,3,256,16]{2,3,1,0:T(8,128)(2,1)}) %all-reduce.2.cloned.1.call-update) | async-done | bytes 98320 | tf_op jit(solution)/shard_map/psum | solution.py:226
  211.7 1.1 broadcast_select_fusion.2
  212.8 11.1 %convolution_convert_fusion = bf16[4,3,256,2048]{3,2,1,0:T(8,128)(2,1)} fusion(bf16[4,3,256,256]{2,3,1,0:T(8,128)(2,1)S(1)} %bitcast.30, bf16[4,3,256,2048]{3,2,1,0:T(8,128)(2,1)} %bitcast.24), kind=kOutput, calls=%fused_computation.4 | convolution fusion | flops 3227516928 | bytes 26738688 | tf_op jit(solution)/shard_map/dot_general | solution.py:229
  223.9 1.6 copy-done.1
  225.5 1.8 copy.18
  227.3 1.9 copy.26
  229.2 166.8 %shard_map.74 = f32[8,512,256]{2,1,0:T(8,128)} custom-call(bf16[512,2048]{1,0:T(8,128)(2,1)} %bitcast.33, bf16[2048,8192]{1,0:T(8,128)(2,1)} %w_hbm.3), custom_call_target="tpu_custom_call" | custom-call | flops 17179869184 | bytes 100663296 | tf_op jit(solution)/shard_map/pallas_call | solution.py:156
  396.0 6.6 %copy.25 = f32[512,8,256]{2,1,0:T(8,128)} copy(f32[512,8,256]{2,0,1:T(8,128)} %bitcast.31) | data formatting | bytes 8388608 | tf_op jit(solution)/shard_map/transpose | solution.py:241
  402.6 4.9 %reshape.45 = f32[2,256,2048]{2,1,0:T(8,128)} reshape(f32[512,8,256]{2,1,0:T(8,128)} %copy.25) | data formatting | bytes 8388608 | tf_op jit(solution)/shard_map/reshape | solution.py:241
  407.4 6.0 %fusion.1 = bf16[3,256,2048]{2,1,0:T(8,128)(2,1)} fusion(f32[2,256,2048]{2,1,0:T(8,128)} %reshape.45, f32[1,256,2048]{2,1,0:T(8,128)S(1)} %copy.26, bf16[1,3,256,2048]{3,2,1,0:T(8,128)(2,1)} %reduce-scatter.2.cloned.1.call-done, bf16[3,256,2048]{2,1,0:T(8,128)(2,1)} %param.10), kind=kLoop, calls=%fused_computation.7 | loop fusion | flops 11010048 | bytes 15728640 | tf_op jit(solution)/shard_map/convert_element_type | solution.py:249
  (20 shorter events, 0.3 us)
Async XLA Ops:
  6.5 159.2 %all-gather.5.cloned.1.call-start = ((), (), s32[]{:S(2)}) async-start(), calls=%async_computation.3 | async-start | bytes 15728640 | tf_op jit(solution)/shard_map/all_gather | solution.py:203
  7.3 204.4 %all-reduce.2.cloned.1.call-start = ((), (), s32[]{:S(2)}) async-start(), calls=%async_computation.1 | async-start | bytes 196608 | tf_op jit(solution)/shard_map/psum | solution.py:226
  30.4 14.3 %copy-start = (bf16[3,256,2048]{2,1,0:T(8,128)(2,1)S(1)}, bf16[3,256,2048]{2,1,0:T(8,128)(2,1)}, u32[]{:S(2)}) copy-start(bf16[3,256,2048]{2,1,0:T(8,128)(2,1)} %param.9) | copy-start | bytes 9437188
  176.9 230.5 %reduce-scatter.2.cloned.1.call-start = ((), (), s32[]{:S(2)}) async-start(), calls=%async_computation.2 | async-start | bytes 15728640 | tf_op jit(solution)/shard_map/reduce_scatter | solution.py:237
  223.9 1.6 copy-start.1
Sparse Core Ops, SparseCore 0:
  8.9 83.1 all-gather.4
  177.0 34.6 all-reduce.1
  224.0 99.0 reduce-scatter.1

commit v2 on v1

--- a/solution.py
+++ b/solution.py
@@ -17,6 +17,7 @@
 ):
     me = lax.axis_index("tensor")
     steps = (n - 1) * per_block
+    skew = 2
 
     def fetch(t):
         return pltpu.make_async_copy(
@@ -78,12 +79,14 @@
         fetch(t).wait()
         part[...] = jnp.dot(a_ref[...], w_buf[t], preferred_element_type=jnp.float32)
 
-    def step(i, carry):
-        right_block, left_block, piece = blocks(i)
-
-        @pl.when(right_block > me)
-        def _():
-            t = right_block * per_block + piece
+    def step(turn, carry):
+        going_right, going_left = turn - me * skew, turn - (n - 1 - me) * skew
+        i = lax.max(going_right, 0)
+        block, piece = n - 1 - i // per_block, i % per_block
+
+        @pl.when((going_right >= 0) & (going_right < steps) & (block > me))
+        def _():
+            t = block * per_block + piece
             product(t)
 
             @pl.when(me > 0)
@@ -94,9 +97,12 @@
             from_left[t] = part[...].astype(jnp.bfloat16)
             send_right(t).start()
 
-        @pl.when(left_block < me)
-        def _():
-            t = left_block * per_block + piece
+        k = lax.max(going_left, 0)
+        other, piece_left = k // per_block, k % per_block
+
+        @pl.when((going_left >= 0) & (going_left < steps) & (other < me))
+        def _():
+            t = other * per_block + piece_left
             product(t)
 
             @pl.when(me < n - 1)
@@ -109,7 +115,7 @@
 
         return carry
 
-    lax.fori_loop(0, steps, step, 0)
+    lax.fori_loop(0, steps + (n - 1) * skew, step, 0)
 
     def own(i, carry):
         t = me * per_block + i
@@ -125,7 +131,7 @@
             send_left(t).wait_recv()
             part[...] += from_right[t].astype(jnp.float32)
 
-        o_ref[i] = part[...]
+        o_ref[:, pl.ds(pl.multiple_of(i * tile, tile), tile)] = part[...]
         return carry
 
     lax.fori_loop(0, per_block, own, 0)
@@ -146,8 +152,8 @@
     lax.fori_loop(0, steps, drain, 0)
 
 
-def project(inputs, weight, n, collective_id):
-    rows, depth = inputs.shape
+def project(inputs, weight, n, at, rows, collective_id):
+    depth = inputs.shape[1]
     columns = weight.shape[1]
     width = columns // n
     tile = min(256, width)
@@ -155,12 +161,13 @@
     tiles = n * per_block
     return pl.pallas_call(
         functools.partial(project_kernel, n, per_block, tile),
-        out_shape=jax.ShapeDtypeStruct((per_block, rows, tile), jnp.float32),
+        out_shape=jax.ShapeDtypeStruct((rows, width), jnp.float32),
+        grid=(1,),
         in_specs=[
-            pl.BlockSpec(memory_space=pltpu.VMEM),
+            pl.BlockSpec((rows, depth), lambda _: (at, 0), pipeline_mode=pl.Buffered(1)),
             pl.BlockSpec(memory_space=pl.ANY),
         ],
-        out_specs=pl.BlockSpec(memory_space=pltpu.VMEM),
+        out_specs=pl.BlockSpec((rows, width), lambda _: (0, 0), pipeline_mode=pl.Buffered(1)),
         scratch_shapes=[
             pltpu.VMEM((tiles, depth, tile), jnp.bfloat16),
             pltpu.VMEM((rows, tile), jnp.float32),
@@ -181,6 +188,63 @@
             transcendentals=0,
         ),
     )(inputs, weight)
+
+
+def owned(slots_ref, columns, rank):
+    column = lax.broadcasted_iota(jnp.int32, (1, columns), 1)
+    mine = slots_ref[0] == column // rank
+    pick = lax.broadcasted_iota(jnp.int32, (rank, columns), 0) == column % rank
+    return mine, pick.astype(jnp.bfloat16)
+
+
+def shrink_kernel(wanted, inputs_ref, slots_ref, *refs):
+    maps, out_ref = refs[:-1], refs[-1]
+    rank = out_ref.shape[1]
+    mine, pick = owned(slots_ref, len(maps) * rank, rank)
+    down = jnp.concatenate([m[0] for m in maps], axis=0)
+    every = lax.dot_general(
+        inputs_ref[0], down, (((1,), (1,)), ((), ())), preferred_element_type=jnp.float32
+    )
+    masked = jnp.where(mine, every, 0.0).astype(jnp.bfloat16)
+    out_ref[0] = lax.dot_general(
+        pick, masked, (((1,), (1,)), ((), ())), preferred_element_type=jnp.float32
+    ).astype(jnp.bfloat16)
+
+
+def expand_kernel(wanted, shrink_ref, slots_ref, *refs):
+    maps, out_ref = refs[:-1], refs[-1]
+    rank = shrink_ref.shape[1]
+    mine, pick = owned(slots_ref, len(maps) * rank, rank)
+    spread = lax.dot_general(
+        shrink_ref[0], pick, (((0,), (0,)), ((), ())), preferred_element_type=jnp.float32
+    )
+    spread = jnp.where(mine, spread, 0.0).astype(jnp.bfloat16)
+    up = jnp.concatenate([m[0] for m in maps], axis=0)
+    out_ref[0] = jnp.dot(spread, up, preferred_element_type=jnp.float32).astype(jnp.bfloat16)
+
+
+def with_adapters(kernel, wanted, operand, slots, maps, out_shape):
+    count, per_owner = wanted.shape
+    rank, width = maps.shape[1:]
+
+    def adapter(j):
+        return pl.BlockSpec((1, rank, width), lambda i, w: (w[i, j], 0, 0))
+
+    def whole(shape):
+        return pl.BlockSpec((1,) + shape[1:], lambda i, w: (i, 0, 0))
+
+    return pl.pallas_call(
+        kernel,
+        out_shape=jax.ShapeDtypeStruct(out_shape, jnp.bfloat16),
+        grid_spec=pltpu.PrefetchScalarGridSpec(
+            num_scalar_prefetch=1,
+            grid=(count,),
+            in_specs=[whole(operand.shape), whole(slots.shape)]
+            + [adapter(j) for j in range(per_owner)],
+            out_specs=whole(out_shape),
+        ),
+        compiler_params=pltpu.CompilerParams(vmem_limit_bytes=48 * 2**20),
+    )(wanted, operand, slots, *([maps] * per_owner))
 
 
 def shards(
@@ -199,54 +263,47 @@
     width = residual.shape[2]
     owners, per_owner = lacking_adapter_lists.shape[2:]
     me = lax.axis_index("dp")
+    batches = groups * step_count
+    rows = step_count * row_count
 
     everyone = lax.all_gather(attention, "dp", axis=0)
     small = jnp.concatenate(
         [lacking_adapter_lists[:, 0].reshape(step_count, -1), request_slot_index], axis=1
     )
     small = lax.all_gather(small, "dp", axis=0)
-    wanted = small[:, :, : owners * per_owner].reshape(groups, step_count, owners, per_owner)
-    wanted = lax.dynamic_index_in_dim(wanted, me, axis=2, keepdims=False)
+    wanted = small[:, :, : owners * per_owner].reshape(batches, owners, per_owner)
+    wanted = lax.dynamic_index_in_dim(wanted, me, axis=1, keepdims=False)
     slots = small[:, :, owners * per_owner :] - me * per_owner
-    down_now = jnp.take(adapter_down_maps, wanted, axis=0).reshape(
-        groups, step_count, per_owner * rank, feature_count
-    )
-    up_now = jnp.take(adapter_up_maps, wanted, axis=0).reshape(
-        groups, step_count, per_owner * rank, width
-    )
-
-    first = project(attention[0], output_weight, n, 1)
-
-    mine = slots[..., None] == jnp.arange(per_owner, dtype=jnp.int32)
+    slots = slots.reshape(batches, row_count, 1)
+
+    flat = attention.reshape(rows, feature_count)
+    first = project(flat, output_weight, n, 0, rows // 3, 1)
     everyone, first = lax.optimization_barrier((everyone, first))
-    shrink_all = lax.dot_general(
-        everyone, down_now, (((3,), (3,)), ((0, 1), (0, 1))), preferred_element_type=jnp.float32
-    ).reshape(groups, step_count, row_count, per_owner, rank)
-    picked = jnp.sum(jnp.where(mine[..., None], shrink_all, 0.0), axis=3)
-    shrink = lax.psum(picked.astype(jnp.bfloat16), "tensor")
-    expanded = jnp.where(mine[..., None], shrink[:, :, :, None, :], jnp.zeros((), jnp.bfloat16))
-    expanded = expanded.reshape(groups, step_count, row_count, per_owner * rank)
-    lora = lax.dot_general(
-        expanded, up_now, (((3,), (2,)), ((0, 1), (0, 1))), preferred_element_type=jnp.float32
-    ).astype(jnp.bfloat16)
-
-    lora, rest_in = lax.optimization_barrier(
-        (lora, attention[1:].reshape((step_count - 1) * row_count, feature_count))
-    )
-    rest = project(rest_in, output_weight, n, 2)
-    lora_own = lax.psum_scatter(lora, "dp", scatter_dimension=0, tiled=False)
-
-    def placed(pieces, steps):
-        per_block, rows, tile = pieces.shape
-        return pieces.transpose(1, 0, 2).reshape(steps, row_count, per_block * tile)
-
-    projected = jnp.concatenate([placed(first, 1), placed(rest, step_count - 1)], axis=0)
+    shrink = with_adapters(
+        shrink_kernel, wanted, everyone.reshape(batches, row_count, feature_count), slots,
+        adapter_down_maps, (batches, rank, row_count),
+    )
+
+    shrink, flat = lax.optimization_barrier((shrink, flat))
+    second = project(flat, output_weight, n, 2, rows // 6, 2)
+    total = lax.psum(shrink, "tensor")
+    total, second = lax.optimization_barrier((total, second))
+    lora = with_adapters(
+        expand_kernel, wanted, total, slots, adapter_up_maps, (batches, row_count, width)
+    )
+
+    lora, flat = lax.optimization_barrier((lora, flat))
+    third = project(flat, output_weight, n, 1, rows // 2, 3)
+    lora_own = lax.psum_scatter(
+        lora.reshape(groups, rows, width), "dp", scatter_dimension=0, tiled=False
+    )
+    projected = jnp.concatenate([first, second, third], axis=0)
     mixed = (
-        residual.astype(jnp.float32)
+        residual.reshape(rows, width).astype(jnp.float32)
         + projected
         + adapter_scale * lora_own.astype(jnp.float32)
     )
-    return mixed.astype(jnp.bfloat16)
+    return mixed.astype(jnp.bfloat16).reshape(residual.shape)
 
 
 def solution(mesh):

time: 420 us -> 301 us (0.72)
  local copies, waits for them, and re-layouts: 50.6 us -> 4.08 us
  waiting for transfers between devices: 34 us -> 0.79 us
  matrix products: 21.1 us -> 0 us
  other arithmetic: 26.5 us -> 14.4 us
  Pallas kernels: 269 us -> 262 us
    pallas_call x2 -> x3, Pallas kernels: 269 us -> 231 us  [project(): pl.pallas_call(functools.partial(project_kernel, n, per_block, tile), out...]
    psum x1, waiting for transfers between devices: 33.3 us -> 0.02 us  [shards(): total = lax.psum(shrink, 'tensor')]
    pallas_call x0 -> x2, Pallas kernels: none -> 31.2 us  [with_adapters(): pl.pallas_call(kernel, out_shape=jax.ShapeDtypeStruct(out_shape, jnp.bflo...]
    gather x2 -> x0, local copies, waits for them, and re-layouts: 30.4 us -> none  [the longest x1 16.2 us: shards(): jnp.take(adapter_up_maps, wanted, axis=0)]
    dot_general x2 -> x0, matrix products: 21.1 us -> none  [the longest x1 11.1 us: shards(): lax.dot_general(expanded, up_now, (((3,), (2,)), ((0, 1), (0, 1))), prefe...]
    select_n x3 -> x0, other arithmetic: 18.5 us -> none  [the longest x1 17.4 us: shards(): jnp.take(adapter_up_maps, wanted, axis=0)]
    transpose x2 -> x0, local copies, waits for them, and re-layouts: 8.37 us -> none  [placed(): return pieces.transpose(1, 0, 2).reshape(steps, row_count, per_block * tile)]
    reshape x3 -> x2, local copies, waits for them, and re-layouts: 6.89 us -> 1.55 us  [the longest x1 1.46 us: shards(): slots = slots.reshape(batches, row_count, 1)]
  transfers between devices with their start and end apart: 3 -> 3, of which waited for: 1 -> 0; matrix products, arithmetic and copies ran while one was open for 16% -> 3% of each run, Pallas kernels for 64% -> 77%
where the time goes in v2:
time: 301 us; the launch traced here: 300 us
  Pallas kernels  262 us (87%)
  other arithmetic  14.4 us (5%)
  between operations  13.2 us (4%)
  blocking collectives  5.18 us (2%)
  local copies, waits for them, and re-layouts  4.08 us (1%)
    pallas_call x3, Pallas kernels, project(): pl.pallas_call(functools.partial(project_kernel, n, per_block, tile), out...  231 us
    pallas_call x2, Pallas kernels, with_adapters(): pl.pallas_call(kernel, out_shape=jax.ShapeDtypeStruct(out_shape, jnp.bflo...  31.2 us
  transfers between devices with their start and end apart: 3, of which 0 were waited for; matrix products, arithmetic and copies ran while one was open for 3% of the time, Pallas kernels for 77%

profile of v2, /device:TPU:16, one launch (start us, length us, event | category | flops | bytes accessed | tf_op | source)
XLA Modules:
  0.0 299.8 jit_solution(14901322856313241633)
XLA Ops:
  6.5 0.0 all-gather.5.cloned.1.call-start
  6.5 0.7 all-gather.5.cloned.1.call-update
  7.3 0.0 all-reduce.2.cloned.1.call-start
  7.3 0.8 reshape_squeeze.3
  8.1 0.8 add_bitcast_fusion
  8.8 5.2 %all-gather.2 = s32[4,3,320]{2,1,0:T(4,128)S(1)} all-gather(s32[1,3,320]{2,1,0:T(4,128)S(1)} %add_bitcast_fusion), channel_id=3, replica_groups=mesh['rep'=2,'dp'=4,'tensor'=4] {'dp'}, dimensions={0}, use_global_device_ids=true | all-gather | bytes 19200 | tf_op jit(solution)/shard_map/all_gather | solution.py:273
  14.0 0.1 reshape.23
  14.1 0.1 slice_subtract_fusion
  14.2 1.5 reshape.32.slots_ref
  15.7 76.6 %shard_map.73 = f32[256,2048]{1,0:T(8,128)} custom-call(bf16[768,2048]{1,0:T(8,128)(2,1)} %bitcast.14, bf16[2048,8192]{1,0:T(8,128)(2,1)} %w_hbm.5), custom_call_target="tpu_custom_call" | custom-call | flops 8589934592 | bytes 67108864 | tf_op jit(solution)/shard_map/pallas_call | solution.py:162
  92.3 0.0 all-gather.5.cloned.1.call-done
  92.3 15.7 %shard_map.74 = bf16[12,16,256]{2,1,0:T(8,128)(2,1)} custom-call(s32[12,16]{1,0:T(8,128)S(1)} %bitcast.11, bf16[12,256,2048]{2,1,0:T(8,128)(2,1)} %all-gather.5.cloned.1.call-done, s32[12,256,1]{2,1,0:T(8,128)S(1)} %reshape.32.slots_ref, bf16[256,16,2048]{2,1,0:T(8,128)(2,1)} %refs_15_.2, bf16[256,16,2048]{2,1,0:T(8,128)(2,1)} %refs_15_.2, ...), custom_call_target="tpu_custom_call" | custom-call | tf_op jit(solution)/shard_map/pallas_call | solution.py:236
  108.0 0.0 all-reduce.2.cloned.1.call-update
  108.0 0.0 reduce-scatter.2.cloned.1.call-start
  108.1 44.7 %shard_map.75 = f32[128,2048]{1,0:T(8,128)} custom-call(bf16[768,2048]{1,0:T(8,128)(2,1)} %bitcast.15, bf16[2048,8192]{1,0:T(8,128)(2,1)} %w_hbm.5), custom_call_target="tpu_custom_call" | custom-call | flops 4294967296 | bytes 50331648 | tf_op jit(solution)/shard_map/pallas_call | solution.py:162
  152.8 0.0 all-reduce.2.cloned.1.call-done.shrink_ref
  152.8 0.9 copy-done
  153.7 15.4 %shard_map.76 = bf16[12,256,2048]{2,1,0:T(8,128)(2,1)} custom-call(s32[12,16]{1,0:T(8,128)S(1)} %bitcast.12, bf16[12,16,256]{2,1,0:T(8,128)(2,1)S(1)} %copy-done, s32[12,256,1]{2,1,0:T(8,128)S(1)} %reshape.32.slots_ref, bf16[256,16,2048]{2,1,0:T(8,128)(2,1)} %refs_15_.3, bf16[256,16,2048]{2,1,0:T(8,128)(2,1)} %refs_15_.3, bf16[256,16,2048]{2,1,0:T(8,128)(2,1)} %refs_15_.3, ...), custom_call_target="tpu_custom_call" | custom-call | tf_op jit(solution)/shard_map/pallas_call | solution.py:236
  169.2 0.0 reduce-scatter.2.cloned.1.call-update
  169.2 109.6 %shard_map.77 = f32[384,2048]{1,0:T(8,128)} custom-call(bf16[768,2048]{1,0:T(8,128)(2,1)} %bitcast.16, bf16[2048,8192]{1,0:T(8,128)(2,1)} %w_hbm.5), custom_call_target="tpu_custom_call" | custom-call | flops 12884901888 | bytes 83886080 | tf_op jit(solution)/shard_map/pallas_call | solution.py:162
  278.8 5.3 %pad_maximum_fusion = f32[768,2048]{1,0:T(8,128)} fusion(f32[384,2048]{1,0:T(8,128)} %shard_map.77, f32[128,2048]{1,0:T(8,128)S(1)} %copy-done.3, f32[256,2048]{1,0:T(8,128)S(1)} %copy-done.2), kind=kLoop, calls=%fused_computation | loop fusion | flops 3145728 | bytes 12582912 | tf_op jit(solution)/shard_map/concatenate | solution.py:300
  284.1 2.9 convert_multiply_fusion
  287.0 0.8 copy-done.1
  287.8 5.4 %add_convert_fusion = bf16[3,256,2048]{2,1,0:T(8,128)(2,1)} fusion(f32[3,256,2048]{2,1,0:T(8,128)S(1)} %bitcast.18, f32[3,256,2048]{2,1,0:T(8,128)S(1)} %bitcast.17, bf16[3,256,2048]{2,1,0:T(8,128)(2,1)} %param.8), kind=kLoop, calls=%fused_computation.1 | loop fusion | flops 6291456 | bytes 18874368 | tf_op jit(solution)/shard_map/convert_element_type | solution.py:306
  (10 shorter events, 0.0 us)
Async XLA Ops:
  6.5 85.8 %all-gather.5.cloned.1.call-start = ((), (), s32[]{:S(2)}) async-start(), calls=%async_computation.3 | async-start | bytes 15728640 | tf_op jit(solution)/shard_map/all_gather | solution.py:269
  7.3 145.6 %all-reduce.2.cloned.1.call-start = ((), (), s32[]{:S(2)}) async-start(), calls=%async_computation.1 | async-start | bytes 196608 | tf_op jit(solution)/shard_map/psum | solution.py:289
  108.0 176.0 %reduce-scatter.2.cloned.1.call-start = ((), (), s32[]{:S(2)}) async-start(), calls=%async_computation.2 | async-start | bytes 15728640 | tf_op jit(solution)/shard_map/reduce_scatter | solution.py:297
  152.8 0.9 copy-start
  169.2 109.6 %copy-start.2 = (f32[256,2048]{1,0:T(8,128)S(1)}, f32[256,2048]{1,0:T(8,128)}, u32[]{:S(2)}) copy-start(f32[256,2048]{1,0:T(8,128)} %shard_map.73) | copy-start | bytes 6291460
  169.2 109.6 %copy-start.3 = (f32[128,2048]{1,0:T(8,128)S(1)}, f32[128,2048]{1,0:T(8,128)}, u32[]{:S(2)}) copy-start(f32[128,2048]{1,0:T(8,128)} %shard_map.75) | copy-start | bytes 3145732
  284.1 3.7 %copy-start.1 = (f32[768,2048]{1,0:T(8,128)S(1)}, f32[768,2048]{1,0:T(8,128)}, u32[]{:S(2)}) copy-start(f32[768,2048]{1,0:T(8,128)} %pad_maximum_fusion) | copy-start | bytes 18874372
Sparse Core Ops, SparseCore 0:
  8.9 83.1 all-gather.4
  108.2 35.2 all-reduce.1
  169.3 98.9 reduce-scatter.1

commit v3 on v2

--- a/solution.py
+++ b/solution.py
@@ -17,7 +17,8 @@
 ):
     me = lax.axis_index("tensor")
     steps = (n - 1) * per_block
-    skew = 2
+    skew, ahead = 2, 3
+    turns = steps + (n - 1) * skew
 
     def fetch(t):
         return pltpu.make_async_copy(
@@ -38,29 +39,28 @@
             device_id={"tensor": me - 1}, device_id_type=MESH,
         )
 
-    def blocks(i):
-        turn, piece = i // per_block, i % per_block
-        return n - 1 - turn, turn, piece
-
-    def fetch_step(i, carry):
-        right_block, left_block, piece = blocks(i)
-
-        @pl.when(right_block > me)
-        def _():
-            fetch(right_block * per_block + piece).start()
-
-        @pl.when(left_block < me)
-        def _():
-            fetch(left_block * per_block + piece).start()
+    def right_flow(turn):
+        going = turn - me * skew
+        i = lax.max(going, 0)
+        block = n - 1 - i // per_block
+        return (going >= 0) & (going < steps) & (block > me), block * per_block + i % per_block
+
+    def left_flow(turn):
+        going = turn - (n - 1 - me) * skew
+        i = lax.max(going, 0)
+        return (going >= 0) & (going < steps) & (i // per_block < me), i
+
+    def fetch_turn(turn, carry):
+        for flow in (right_flow, left_flow):
+            active, t = flow(turn)
+
+            @pl.when(active)
+            def _():
+                fetch(t).start()
 
         return carry
 
-    def fetch_own(i, carry):
-        fetch(me * per_block + i).start()
-        return carry
-
-    lax.fori_loop(0, steps, fetch_step, 0)
-    lax.fori_loop(0, per_block, fetch_own, 0)
+    lax.fori_loop(0, ahead, fetch_turn, 0)
 
     barrier = pltpu.get_barrier_semaphore()
 
@@ -80,13 +80,16 @@
         part[...] = jnp.dot(a_ref[...], w_buf[t], preferred_element_type=jnp.float32)
 
     def step(turn, carry):
-        going_right, going_left = turn - me * skew, turn - (n - 1 - me) * skew
-        i = lax.max(going_right, 0)
-        block, piece = n - 1 - i // per_block, i % per_block
-
-        @pl.when((going_right >= 0) & (going_right < steps) & (block > me))
-        def _():
-            t = block * per_block + piece
+        fetch_turn(turn + ahead, 0)
+
+        @pl.when(turn < per_block)
+        def _():
+            fetch(me * per_block + turn).start()
+
+        active, t = right_flow(turn)
+
+        @pl.when(active)
+        def _():
             product(t)
 
             @pl.when(me > 0)
@@ -97,25 +100,23 @@
             from_left[t] = part[...].astype(jnp.bfloat16)
             send_right(t).start()
 
-        k = lax.max(going_left, 0)
-        other, piece_left = k // per_block, k % per_block
-
-        @pl.when((going_left >= 0) & (going_left < steps) & (other < me))
-        def _():
-            t = other * per_block + piece_left
-            product(t)
+        other, u = left_flow(turn)
+
+        @pl.when(other)
+        def _():
+            product(u)
 
             @pl.when(me < n - 1)
             def _():
-                send_left(t).wait_recv()
-                part[...] += from_right[t].astype(jnp.float32)
-
-            from_right[t] = part[...].astype(jnp.bfloat16)
-            send_left(t).start()
+                send_left(u).wait_recv()
+                part[...] += from_right[u].astype(jnp.float32)
+
+            from_right[u] = part[...].astype(jnp.bfloat16)
+            send_left(u).start()
 
         return carry
 
-    lax.fori_loop(0, steps + (n - 1) * skew, step, 0)
+    lax.fori_loop(0, turns, step, 0)
 
     def own(i, carry):
         t = me * per_block + i
@@ -136,20 +137,22 @@
 
     lax.fori_loop(0, per_block, own, 0)
 
-    def drain(i, carry):
-        right_block, left_block, piece = blocks(i)
-
-        @pl.when(right_block > me)
-        def _():
-            send_right(right_block * per_block + piece).wait_send()
-
-        @pl.when(left_block < me)
-        def _():
-            send_left(left_block * per_block + piece).wait_send()
+    def drain(turn, carry):
+        active, t = right_flow(turn)
+
+        @pl.when(active)
+        def _():
+            send_right(t).wait_send()
+
+        other, u = left_flow(turn)
+
+        @pl.when(other)
+        def _():
+            send_left(u).wait_send()
 
         return carry
 
-    lax.fori_loop(0, steps, drain, 0)
+    lax.fori_loop(0, turns, drain, 0)
 
 
 def project(inputs, weight, n, at, rows, collective_id):
@@ -197,11 +200,38 @@
     return mine, pick.astype(jnp.bfloat16)
 
 
-def shrink_kernel(wanted, inputs_ref, slots_ref, *refs):
-    maps, out_ref = refs[:-1], refs[-1]
-    rank = out_ref.shape[1]
-    mine, pick = owned(slots_ref, len(maps) * rank, rank)
-    down = jnp.concatenate([m[0] for m in maps], axis=0)
+def fetched(wanted, maps_hbm, held, sems):
+    i, count = pl.program_id(0), pl.num_programs(0)
+    slots, rank = held.shape[0], maps_hbm.shape[1]
+
+    def copies(step):
+        slot = lax.rem(step, slots)
+        return [
+            pltpu.make_async_copy(
+                maps_hbm.at[wanted[step, j]], held.at[slot, pl.ds(j * rank, rank)], sems.at[slot, j]
+            )
+            for j in range(wanted.shape[1])
+        ]
+
+    @pl.when(i == 0)
+    def _():
+        for step in range(slots - 1):
+            for copy in copies(step):
+                copy.start()
+
+    @pl.when(i + slots - 1 < count)
+    def _():
+        for copy in copies(i + slots - 1):
+            copy.start()
+
+    for copy in copies(i):
+        copy.wait()
+    return held[lax.rem(i, slots)]
+
+
+def shrink_kernel(wanted, inputs_ref, slots_ref, maps_hbm, out_ref, held, sems):
+    mine, pick = owned(slots_ref, held.shape[1], out_ref.shape[1])
+    down = fetched(wanted, maps_hbm, held, sems)
     every = lax.dot_general(
         inputs_ref[0], down, (((1,), (1,)), ((), ())), preferred_element_type=jnp.float32
     )
@@ -211,24 +241,20 @@
     ).astype(jnp.bfloat16)
 
 
-def expand_kernel(wanted, shrink_ref, slots_ref, *refs):
-    maps, out_ref = refs[:-1], refs[-1]
-    rank = shrink_ref.shape[1]
-    mine, pick = owned(slots_ref, len(maps) * rank, rank)
+def expand_kernel(wanted, shrink_ref, slots_ref, maps_hbm, out_ref, held, sems):
+    mine, pick = owned(slots_ref, held.shape[1], shrink_ref.shape[1])
     spread = lax.dot_general(
         shrink_ref[0], pick, (((0,), (0,)), ((), ())), preferred_element_type=jnp.float32
     )
     spread = jnp.where(mine, spread, 0.0).astype(jnp.bfloat16)
-    up = jnp.concatenate([m[0] for m in maps], axis=0)
+    up = fetched(wanted, maps_hbm, held, sems)
     out_ref[0] = jnp.dot(spread, up, preferred_element_type=jnp.float32).astype(jnp.bfloat16)
 
 
 def with_adapters(kernel, wanted, operand, slots, maps, out_shape):
     count, per_owner = wanted.shape
     rank, width = maps.shape[1:]
-
-    def adapter(j):
-        return pl.BlockSpec((1, rank, width), lambda i, w: (w[i, j], 0, 0))
+    depth = min(4, count)
 
     def whole(shape):
         return pl.BlockSpec((1,) + shape[1:], lambda i, w: (i, 0, 0))
@@ -239,12 +265,51 @@
         grid_spec=pltpu.PrefetchScalarGridSpec(
             num_scalar_prefetch=1,
             grid=(count,),
-            in_specs=[whole(operand.shape), whole(slots.shape)]
-            + [adapter(j) for j in range(per_owner)],
+            in_specs=[
+                whole(operand.shape), whole(slots.shape), pl.BlockSpec(memory_space=pl.ANY),
+            ],
             out_specs=whole(out_shape),
+            scratch_shapes=[
+                pltpu.VMEM((depth, per_owner * rank, width), jnp.bfloat16),
+                pltpu.SemaphoreType.DMA((depth, per_owner)),
+            ],
         ),
         compiler_params=pltpu.CompilerParams(vmem_limit_bytes=48 * 2**20),
-    )(wanted, operand, slots, *([maps] * per_owner))
+    )(wanted, operand, slots, maps)
+
+
+def mix_kernel(residual_ref, lora_ref, first_ref, second_ref, third_ref, out_ref):
+    i = pl.program_id(0)
+
+    def mix(projected_ref):
+        out_ref[...] = (
+            residual_ref[...].astype(jnp.float32)
+            + projected_ref[...]
+            + adapter_scale * lora_ref[...].astype(jnp.float32)
+        ).astype(jnp.bfloat16)
+
+    pl.when(i < 2)(lambda: mix(first_ref))
+    pl.when(i == 2)(lambda: mix(second_ref))
+    pl.when(i > 2)(lambda: mix(third_ref))
+
+
+def mix(residual, lora, first, second, third):
+    rows, width = residual.shape
+    block = (rows // 6, width)
+    return pl.pallas_call(
+        mix_kernel,
+        out_shape=jax.ShapeDtypeStruct((rows, width), jnp.bfloat16),
+        grid=(6,),
+        in_specs=[
+            pl.BlockSpec(block, lambda i: (i, 0)),
+            pl.BlockSpec(block, lambda i: (i, 0)),
+            pl.BlockSpec(block, lambda i: (jnp.minimum(i, 1), 0)),
+            pl.BlockSpec(block, lambda i: (0, 0)),
+            pl.BlockSpec(block, lambda i: (jnp.maximum(i - 3, 0), 0)),
+        ],
+        out_specs=pl.BlockSpec(block, lambda i: (i, 0)),
+        compiler_params=pltpu.CompilerParams(vmem_limit_bytes=48 * 2**20),
+    )(residual, lora, first, second, third)
 
 
 def shards(
@@ -270,7 +335,13 @@
     small = jnp.concatenate(
         [lacking_adapter_lists[:, 0].reshape(step_count, -1), request_slot_index], axis=1
     )
-    small = lax.all_gather(small, "dp", axis=0)
+    group = jnp.arange(groups, dtype=jnp.int32)[:, None, None]
+    gathered = jnp.where(group == me, small[None], 0)
+    for shift in range(1, groups):
+        ring = [(i, (i + shift) % groups) for i in range(groups)]
+        passed = lax.ppermute(small, "dp", ring)
+        gathered = jnp.where(group == (me + groups - shift) % groups, passed[None], gathered)
+    small = gathered
     wanted = small[:, :, : owners * per_owner].reshape(batches, owners, per_owner)
     wanted = lax.dynamic_index_in_dim(wanted, me, axis=1, keepdims=False)
     slots = small[:, :, owners * per_owner :] - me * per_owner
@@ -297,13 +368,8 @@
     lora_own = lax.psum_scatter(
         lora.reshape(groups, rows, width), "dp", scatter_dimension=0, tiled=False
     )
-    projected = jnp.concatenate([first, second, third], axis=0)
-    mixed = (
-        residual.reshape(rows, width).astype(jnp.float32)
-        + projected
-        + adapter_scale * lora_own.astype(jnp.float32)
-    )
-    return mixed.astype(jnp.bfloat16).reshape(residual.shape)
+    mixed = mix(residual.reshape(rows, width), lora_own, first, second, third)
+    return mixed.reshape(residual.shape)
 
 
 def solution(mesh):

time: 301 us -> 292 us (0.970)
  other arithmetic: 14.4 us -> 0.25 us
  blocking collectives: 5.18 us -> 0 us
  Pallas kernels: 262 us -> 267 us
  waiting for transfers between devices: 0.79 us -> 5.4 us
    pallas_call x0 -> x1, Pallas kernels: none -> 7.2 us  [mix(): pl.pallas_call(mix_kernel, out_shape=jax.ShapeDtypeStruct((rows, width),...]
    convert_element_type x1 -> x0, other arithmetic: 5.44 us -> none  [shards(): return mixed.astype(jnp.bfloat16).reshape(residual.shape)]
    concatenate x1, other arithmetic: 5.29 us -> 0.07 us  [shards(): jnp.concatenate([lacking_adapter_lists[:, 0].reshape(step_count, -1), req...]
    all_gather x1 -> x0, blocking collectives: 5.18 us -> none  [shards(): small = lax.all_gather(small, 'dp', axis=0)]
    all_gather x1, waiting for transfers between devices: 0.02 us -> 4.6 us  [shards(): everyone = lax.all_gather(attention, 'dp', axis=0)]
  transfers between devices with their start and end apart: 3 -> 6, of which waited for: 0 -> 1; matrix products, arithmetic and copies ran while one was open for 3% -> 1% of each run, Pallas kernels for 77% -> 79%
where the time goes in v3:
time: 292 us; the launch traced here: 291 us
  Pallas kernels  267 us (91%)
  between operations  13.3 us (5%)
  waiting for transfers between devices  5.4 us (2%)
  starting transfers between devices  3.04 us (1%)
    pallas_call x3, Pallas kernels, project(): pl.pallas_call(functools.partial(project_kernel, n, per_block, tile), out...  230 us
    pallas_call x2, Pallas kernels, with_adapters(): pl.pallas_call(kernel, out_shape=jax.ShapeDtypeStruct(out_shape, jnp.bflo...  29.6 us
    pallas_call x1, Pallas kernels, mix(): pl.pallas_call(mix_kernel, out_shape=jax.ShapeDtypeStruct((rows, width),...  7.2 us
  transfers between devices with their start and end apart: 6, of which 1 were waited for; matrix products, arithmetic and copies ran while one was open for 1% of the time, Pallas kernels for 79%

profile of v3, /device:TPU:16, one launch (start us, length us, event | category | flops | bytes accessed | tf_op | source)
XLA Modules:
  0.0 291.1 jit_solution(6432100761155671935)
XLA Ops:
  6.5 0.7 all-gather.3.cloned.1.call-update
  7.3 0.0 all-reduce.2.cloned.1.call-start
  7.3 0.1 reshape_squeeze.3
  7.4 0.1 pad_add_fusion
  7.5 0.0 collective-permute-start.2
  7.5 1.6 collective-permute-start.1
  9.0 1.4 collective-permute-start
  10.4 75.3 %shard_map.73.first_ref = f32[256,2048]{1,0:T(8,128)} custom-call(bf16[768,2048]{1,0:T(8,128)(2,1)} %bitcast.13, bf16[2048,8192]{1,0:T(8,128)(2,1)} %w_hbm.5), custom_call_target="tpu_custom_call" | custom-call | flops 8589934592 | bytes 67108864 | tf_op jit(solution)/shard_map/pallas_call | solution.py:165
  85.8 0.1 select_select_fusion
  85.9 0.1 reshape.46
  86.0 0.1 slice_subtract_fusion
  86.1 1.5 reshape.53.slots_ref
  87.5 4.6 %all-gather.3.cloned.1.call-done = bf16[12,256,2048]{2,1,0:T(8,128)(2,1)} async-done(((bf16[3,256,2048]{2,1,0:T(8,128)(2,1)}), bf16[12,256,2048]{2,1,0:T(8,128)(2,1)}) %all-gather.3.cloned.1.call-update) | async-done | bytes 12582928 | tf_op jit(solution)/shard_map/all_gather | solution.py:334
  92.1 16.2 %shard_map.74 = bf16[12,16,256]{2,1,0:T(8,128)(2,1)} custom-call(s32[12,16]{1,0:T(8,128)S(1)} %bitcast.10, bf16[12,256,2048]{2,1,0:T(8,128)(2,1)} %all-gather.3.cloned.1.call-done, s32[12,256,1]{2,1,0:T(8,128)S(1)} %reshape.53.slots_ref, bf16[256,16,2048]{2,1,0:T(8,128)(2,1)} %maps_hbm.2), custom_call_target="tpu_custom_call" | custom-call | tf_op jit(solution)/shard_map/pallas_call | solution.py:262
  108.4 0.0 all-reduce.2.cloned.1.call-update
  108.4 0.0 reduce-scatter.2.cloned.1.call-start
  108.4 45.1 %shard_map.75.second_ref = f32[128,2048]{1,0:T(8,128)} custom-call(bf16[768,2048]{1,0:T(8,128)(2,1)} %bitcast.14, bf16[2048,8192]{1,0:T(8,128)(2,1)} %w_hbm.5), custom_call_target="tpu_custom_call" | custom-call | flops 4294967296 | bytes 50331648 | tf_op jit(solution)/shard_map/pallas_call | solution.py:165
  153.5 0.0 all-reduce.2.cloned.1.call-done.shrink_ref
  153.6 0.9 copy-done.2
  154.5 13.4 %shard_map.76 = bf16[12,256,2048]{2,1,0:T(8,128)(2,1)} custom-call(s32[12,16]{1,0:T(8,128)S(1)} %bitcast.11, bf16[12,16,256]{2,1,0:T(8,128)(2,1)S(1)} %copy-done.2, s32[12,256,1]{2,1,0:T(8,128)S(1)} %reshape.53.slots_ref, bf16[256,16,2048]{2,1,0:T(8,128)(2,1)} %maps_hbm.3), custom_call_target="tpu_custom_call" | custom-call | tf_op jit(solution)/shard_map/pallas_call | solution.py:262
  167.9 0.0 reduce-scatter.2.cloned.1.call-update
  167.9 109.4 %shard_map.77.third_ref = f32[384,2048]{1,0:T(8,128)} custom-call(bf16[768,2048]{1,0:T(8,128)(2,1)} %bitcast.15, bf16[2048,8192]{1,0:T(8,128)(2,1)} %w_hbm.5), custom_call_target="tpu_custom_call" | custom-call | flops 12884901888 | bytes 83886080 | tf_op jit(solution)/shard_map/pallas_call | solution.py:165
  277.3 0.0 reduce-scatter.2.cloned.1.call-done
  277.4 7.2 %shard_map.78 = bf16[768,2048]{1,0:T(8,128)(2,1)} custom-call(bf16[768,2048]{1,0:T(8,128)(2,1)} %bitcast.16, bf16[768,2048]{1,0:T(8,128)(2,1)} %bitcast.17, f32[256,2048]{1,0:T(8,128)S(1)} %copy-done, f32[128,2048]{1,0:T(8,128)S(1)} %copy-done.1, f32[384,2048]{1,0:T(8,128)} %shard_map.77.third_ref), custom_call_target="tpu_custom_call" | custom-call | tf_op jit(solution)/shard_map/pallas_call | solution.py:299
  (18 shorter events, 0.1 us)
Async XLA Ops:
  6.5 0.8 copy-start.3
  6.5 0.9 copy-start.4
  6.5 85.6 %all-gather.3.cloned.1.call-start = ((), (), s32[]{:S(2)}) async-start(), calls=%async_computation.3 | async-start | bytes 15728640 | tf_op jit(solution)/shard_map/all_gather | solution.py:334
  7.3 146.3 %all-reduce.2.cloned.1.call-start = ((), (), s32[]{:S(2)}) async-start(), calls=%async_computation.1 | async-start | bytes 196608 | tf_op jit(solution)/shard_map/psum | solution.py:360
  7.5 78.3 %collective-permute-start.2 = (s32[3,320]{1,0:T(4,128)S(1)}, s32[3,320]{1,0:T(4,128)S(1)}, u32[]{:S(2)}, u32[]{:S(2)}) collective-permute-start(s32[3,320]{1,0:T(4,128)S(1)} %pad_add_fusion), channel_id=1, source_target_pairs={{0,4},{4,8},{8,12},{12,0},{1,5},{5,9},{9,13},{13,1},{2,6},{6,10},{... | collective-permute-start | bytes 11528 | tf_op jit(solution)/shard_map/ppermute | solution.py:342
  7.5 78.3 %collective-permute-start.1 = (s32[3,320]{1,0:T(4,128)S(1)}, s32[3,320]{1,0:T(4,128)S(1)}, u32[]{:S(2)}, u32[]{:S(2)}) collective-permute-start(s32[3,320]{1,0:T(4,128)S(1)} %pad_add_fusion), channel_id=1, source_target_pairs={{0,8},{4,12},{8,0},{12,4},{1,9},{5,13},{9,1},{13,5},{2,10},{6,14},... | collective-permute-start | bytes 11528 | tf_op jit(solution)/shard_map/ppermute | solution.py:342
  9.0 76.7 %collective-permute-start = (s32[3,320]{1,0:T(4,128)S(1)}, s32[3,320]{1,0:T(4,128)S(1)}, u32[]{:S(2)}, u32[]{:S(2)}) collective-permute-start(s32[3,320]{1,0:T(4,128)S(1)} %pad_add_fusion), channel_id=1, source_target_pairs={{0,12},{4,0},{8,4},{12,8},{1,13},{5,1},{9,5},{13,9},{2,14},{6,2},{... | collective-permute-start | bytes 11528 | tf_op jit(solution)/shard_map/ppermute | solution.py:342
  108.4 169.0 %reduce-scatter.2.cloned.1.call-start = ((), (), s32[]{:S(2)}) async-start(), calls=%async_computation.2 | async-start | bytes 15728640 | tf_op jit(solution)/shard_map/reduce_scatter | solution.py:368
  153.6 0.9 copy-start.2
  167.9 109.5 %copy-start = (f32[256,2048]{1,0:T(8,128)S(1)}, f32[256,2048]{1,0:T(8,128)}, u32[]{:S(2)}) copy-start(f32[256,2048]{1,0:T(8,128)} %shard_map.73.first_ref) | copy-start | bytes 6291460
  167.9 109.5 %copy-start.1 = (f32[128,2048]{1,0:T(8,128)S(1)}, f32[128,2048]{1,0:T(8,128)}, u32[]{:S(2)}) copy-start(f32[128,2048]{1,0:T(8,128)} %shard_map.75.second_ref) | copy-start | bytes 3145732
Sparse Core Ops, SparseCore 0:
  8.9 83.1 all-gather.2
  108.5 34.9 all-reduce.1
  168.0 98.3 reduce-scatter.1

commit v4 on v3

--- a/solution.py
+++ b/solution.py
@@ -1,4 +1,5 @@
 import functools
+import math
 
 import jax
 import jax.numpy as jnp
@@ -12,8 +13,8 @@
 
 
 def project_kernel(
-    n, per_block, tile, a_ref, w_hbm, o_ref, w_buf, part, from_left, from_right,
-    w_sem, left_sem, right_sem, to_right_sem, to_left_sem,
+    n, per_block, tile, start, a_hbm, w_hbm, o_ref, a_ref, w_buf, part, from_left, from_right,
+    a_sem, w_sem, left_sem, right_sem, to_right_sem, to_left_sem,
 ):
     me = lax.axis_index("tensor")
     steps = (n - 1) * per_block
@@ -60,6 +61,8 @@
 
         return carry
 
+    inputs = pltpu.make_async_copy(a_hbm.at[pl.ds(start, a_ref.shape[0])], a_ref, a_sem)
+    inputs.start()
     lax.fori_loop(0, ahead, fetch_turn, 0)
 
     barrier = pltpu.get_barrier_semaphore()
@@ -74,6 +77,7 @@
 
     peers = (me > 0).astype(jnp.int32) + (me < n - 1).astype(jnp.int32)
     pl.semaphore_wait(barrier, peers)
+    inputs.wait()
 
     def product(t):
         fetch(t).wait()
@@ -155,7 +159,7 @@
     lax.fori_loop(0, turns, drain, 0)
 
 
-def project(inputs, weight, n, at, rows, collective_id):
+def project(inputs, weight, n, start, rows, collective_id):
     depth = inputs.shape[1]
     columns = weight.shape[1]
     width = columns // n
@@ -163,19 +167,17 @@
     per_block = width // tile
     tiles = n * per_block
     return pl.pallas_call(
-        functools.partial(project_kernel, n, per_block, tile),
+        functools.partial(project_kernel, n, per_block, tile, start),
         out_shape=jax.ShapeDtypeStruct((rows, width), jnp.float32),
-        grid=(1,),
-        in_specs=[
-            pl.BlockSpec((rows, depth), lambda _: (at, 0), pipeline_mode=pl.Buffered(1)),
-            pl.BlockSpec(memory_space=pl.ANY),
-        ],
-        out_specs=pl.BlockSpec((rows, width), lambda _: (0, 0), pipeline_mode=pl.Buffered(1)),
+        in_specs=[pl.BlockSpec(memory_space=pl.ANY)] * 2,
+        out_specs=pl.BlockSpec(memory_space=pltpu.VMEM),
         scratch_shapes=[
+            pltpu.VMEM((rows, depth), jnp.bfloat16),
             pltpu.VMEM((tiles, depth, tile), jnp.bfloat16),
             pltpu.VMEM((rows, tile), jnp.float32),
             pltpu.VMEM((tiles, rows, tile), jnp.bfloat16),
             pltpu.VMEM((tiles, rows, tile), jnp.bfloat16),
+            pltpu.SemaphoreType.DMA,
             pltpu.SemaphoreType.DMA((tiles,)),
             pltpu.SemaphoreType.DMA((tiles,)),
             pltpu.SemaphoreType.DMA((tiles,)),
@@ -278,7 +280,7 @@
     )(wanted, operand, slots, maps)
 
 
-def mix_kernel(residual_ref, lora_ref, first_ref, second_ref, third_ref, out_ref):
+def mix_kernel(ends, residual_ref, lora_ref, first_ref, second_ref, third_ref, out_ref):
     i = pl.program_id(0)
 
     def mix(projected_ref):
@@ -288,28 +290,30 @@
             + adapter_scale * lora_ref[...].astype(jnp.float32)
         ).astype(jnp.bfloat16)
 
-    pl.when(i < 2)(lambda: mix(first_ref))
-    pl.when(i == 2)(lambda: mix(second_ref))
-    pl.when(i > 2)(lambda: mix(third_ref))
-
-
-def mix(residual, lora, first, second, third):
+    pl.when(i < ends[0])(lambda: mix(first_ref))
+    pl.when((i >= ends[0]) & (i < ends[1]))(lambda: mix(second_ref))
+    pl.when(i >= ends[1])(lambda: mix(third_ref))
+
+
+def mix(residual, lora, *pieces):
     rows, width = residual.shape
-    block = (rows // 6, width)
+    size = math.gcd(*(piece.shape[0] for piece in pieces))
+    block = (size, width)
+    counts = [piece.shape[0] // size for piece in pieces]
+    starts = [0, counts[0], counts[0] + counts[1]]
+
+    def of_piece(start, count):
+        return pl.BlockSpec(block, lambda i: (jnp.clip(i - start, 0, count - 1), 0))
+
     return pl.pallas_call(
-        mix_kernel,
+        functools.partial(mix_kernel, starts[1:]),
         out_shape=jax.ShapeDtypeStruct((rows, width), jnp.bfloat16),
-        grid=(6,),
-        in_specs=[
-            pl.BlockSpec(block, lambda i: (i, 0)),
-            pl.BlockSpec(block, lambda i: (i, 0)),
-            pl.BlockSpec(block, lambda i: (jnp.minimum(i, 1), 0)),
-            pl.BlockSpec(block, lambda i: (0, 0)),
-            pl.BlockSpec(block, lambda i: (jnp.maximum(i - 3, 0), 0)),
-        ],
+        grid=(rows // size,),
+        in_specs=[pl.BlockSpec(block, lambda i: (i, 0))] * 2
+        + [of_piece(start, count) for start, count in zip(starts, counts)],
         out_specs=pl.BlockSpec(block, lambda i: (i, 0)),
         compiler_params=pltpu.CompilerParams(vmem_limit_bytes=48 * 2**20),
-    )(residual, lora, first, second, third)
+    )(residual, lora, *pieces)
 
 
 def shards(
@@ -347,8 +351,9 @@
     slots = small[:, :, owners * per_owner :] - me * per_owner
     slots = slots.reshape(batches, row_count, 1)
 
+    ends = rows * 3 // 8 // 32 * 32, rows * 13 // 24 // 32 * 32
     flat = attention.reshape(rows, feature_count)
-    first = project(flat, output_weight, n, 0, rows // 3, 1)
+    first = project(flat, output_weight, n, 0, ends[0], 1)
     everyone, first = lax.optimization_barrier((everyone, first))
     shrink = with_adapters(
         shrink_kernel, wanted, everyone.reshape(batches, row_count, feature_count), slots,
@@ -356,7 +361,7 @@
     )
 
     shrink, flat = lax.optimization_barrier((shrink, flat))
-    second = project(flat, output_weight, n, 2, rows // 6, 2)
+    second = project(flat, output_weight, n, ends[0], ends[1] - ends[0], 2)
     total = lax.psum(shrink, "tensor")
     total, second = lax.optimization_barrier((total, second))
     lora = with_adapters(
@@ -364,7 +369,7 @@
     )
 
     lora, flat = lax.optimization_barrier((lora, flat))
-    third = project(flat, output_weight, n, 1, rows // 2, 3)
+    third = project(flat, output_weight, n, ends[1], rows - ends[1], 3)
     lora_own = lax.psum_scatter(
         lora.reshape(groups, rows, width), "dp", scatter_dimension=0, tiled=False
     )

time: 292 us -> 292 us (level)
    all_gather x1, waiting for transfers between devices: 4.6 us -> 0.02 us  [shards(): everyone = lax.all_gather(attention, 'dp', axis=0)]
  transfers between devices with their start and end apart: 6 -> 6, of which waited for: 1 -> 1; matrix products, arithmetic and copies ran while one was open for 1% -> 1% of each run, Pallas kernels for 79% -> 77%
where the time goes in v4:
time: 292 us; the launch traced here: 289 us
  Pallas kernels  267 us (91%)
  between operations  13.3 us (5%)
  waiting for transfers between devices  3.36 us (1%)
  starting transfers between devices  3.04 us (1%)
    pallas_call x3, Pallas kernels, project(): pl.pallas_call(functools.partial(project_kernel, n, per_block, tile, star...  222 us
    pallas_call x2, Pallas kernels, with_adapters(): pl.pallas_call(kernel, out_shape=jax.ShapeDtypeStruct(out_shape, jnp.bflo...  29.7 us
    pallas_call x1, Pallas kernels, mix(): pl.pallas_call(functools.partial(mix_kernel, starts[1:]), out_shape=jax.S...  15.2 us
  transfers between devices with their start and end apart: 6, of which 1 were waited for; matrix products, arithmetic and copies ran while one was open for 1% of the time, Pallas kernels for 77%

profile of v4, /device:TPU:16, one launch (start us, length us, event | category | flops | bytes accessed | tf_op | source)
XLA Modules:
  0.0 289.1 jit_solution(12808880347257661356)
XLA Ops:
  6.5 0.7 all-gather.3.cloned.1.call-update
  7.3 0.0 all-reduce.2.cloned.1.call-start
  7.3 0.1 reshape_squeeze.3
  7.4 0.1 pad_add_fusion
  7.5 0.0 collective-permute-start.2
  7.5 1.6 collective-permute-start.1
  9.0 1.4 collective-permute-start
  10.4 83.0 %shard_map.73.first_ref = f32[288,2048]{1,0:T(8,128)} custom-call(bf16[768,2048]{1,0:T(8,128)(2,1)} %bitcast.13, bf16[2048,8192]{1,0:T(8,128)(2,1)} %w_hbm.5), custom_call_target="tpu_custom_call" | custom-call | flops 9663676416 | bytes 71303168 | tf_op jit(solution)/shard_map/pallas_call | solution.py:169
  93.5 0.1 select_select_fusion
  93.6 0.1 reshape.46
  93.7 0.1 slice_subtract_fusion
  93.7 1.5 reshape.53.slots_ref
  95.2 0.0 all-gather.3.cloned.1.call-done
  95.2 16.2 %shard_map.74 = bf16[12,16,256]{2,1,0:T(8,128)(2,1)} custom-call(s32[12,16]{1,0:T(8,128)S(1)} %bitcast.10, bf16[12,256,2048]{2,1,0:T(8,128)(2,1)} %all-gather.3.cloned.1.call-done, s32[12,256,1]{2,1,0:T(8,128)S(1)} %reshape.53.slots_ref, bf16[256,16,2048]{2,1,0:T(8,128)(2,1)} %maps_hbm.2), custom_call_target="tpu_custom_call" | custom-call | tf_op jit(solution)/shard_map/pallas_call | solution.py:264
  111.5 0.0 all-reduce.2.cloned.1.call-update
  111.5 0.0 reduce-scatter.2.cloned.1.call-start
  111.5 41.5 %shard_map.75.second_ref = f32[128,2048]{1,0:T(8,128)} custom-call(bf16[768,2048]{1,0:T(8,128)(2,1)} %bitcast.14, bf16[2048,8192]{1,0:T(8,128)(2,1)} %w_hbm.5), custom_call_target="tpu_custom_call" | custom-call | flops 4294967296 | bytes 50331648 | tf_op jit(solution)/shard_map/pallas_call | solution.py:169
  153.1 0.0 all-reduce.2.cloned.1.call-done.shrink_ref
  153.1 0.9 copy-done.2
  154.0 13.5 %shard_map.76 = bf16[12,256,2048]{2,1,0:T(8,128)(2,1)} custom-call(s32[12,16]{1,0:T(8,128)S(1)} %bitcast.11, bf16[12,16,256]{2,1,0:T(8,128)(2,1)S(1)} %copy-done.2, s32[12,256,1]{2,1,0:T(8,128)S(1)} %reshape.53.slots_ref, bf16[256,16,2048]{2,1,0:T(8,128)(2,1)} %maps_hbm.3), custom_call_target="tpu_custom_call" | custom-call | tf_op jit(solution)/shard_map/pallas_call | solution.py:264
  167.5 0.0 reduce-scatter.2.cloned.1.call-update
  167.6 97.2 %shard_map.77.third_ref = f32[352,2048]{1,0:T(8,128)} custom-call(bf16[768,2048]{1,0:T(8,128)(2,1)} %bitcast.15, bf16[2048,8192]{1,0:T(8,128)(2,1)} %w_hbm.5), custom_call_target="tpu_custom_call" | custom-call | flops 11811160064 | bytes 79691776 | tf_op jit(solution)/shard_map/pallas_call | solution.py:169
  264.8 2.6 reduce-scatter.2.cloned.1.call-done
  267.4 15.2 %shard_map.78 = bf16[768,2048]{1,0:T(8,128)(2,1)} custom-call(bf16[768,2048]{1,0:T(8,128)(2,1)} %bitcast.16, bf16[768,2048]{1,0:T(8,128)(2,1)} %bitcast.17, f32[288,2048]{1,0:T(8,128)S(1)} %copy-done, f32[128,2048]{1,0:T(8,128)S(1)} %copy-done.1, f32[352,2048]{1,0:T(8,128)} %shard_map.77.third_ref), custom_call_target="tpu_custom_call" | custom-call | tf_op jit(solution)/shard_map/pallas_call | solution.py:308
  (18 shorter events, 0.1 us)
Async XLA Ops:
  6.5 0.8 copy-start.3
  6.5 0.9 copy-start.4
  6.5 88.7 %all-gather.3.cloned.1.call-start = ((), (), s32[]{:S(2)}) async-start(), calls=%async_computation.3 | async-start | bytes 15728640 | tf_op jit(solution)/shard_map/all_gather | solution.py:338
  7.3 145.8 %all-reduce.2.cloned.1.call-start = ((), (), s32[]{:S(2)}) async-start(), calls=%async_computation.1 | async-start | bytes 196608 | tf_op jit(solution)/shard_map/psum | solution.py:365
  7.5 85.9 %collective-permute-start.2 = (s32[3,320]{1,0:T(4,128)S(1)}, s32[3,320]{1,0:T(4,128)S(1)}, u32[]{:S(2)}, u32[]{:S(2)}) collective-permute-start(s32[3,320]{1,0:T(4,128)S(1)} %pad_add_fusion), channel_id=1, source_target_pairs={{0,4},{4,8},{8,12},{12,0},{1,5},{5,9},{9,13},{13,1},{2,6},{6,10},{... | collective-permute-start | bytes 11528 | tf_op jit(solution)/shard_map/ppermute | solution.py:346
  7.5 86.0 %collective-permute-start.1 = (s32[3,320]{1,0:T(4,128)S(1)}, s32[3,320]{1,0:T(4,128)S(1)}, u32[]{:S(2)}, u32[]{:S(2)}) collective-permute-start(s32[3,320]{1,0:T(4,128)S(1)} %pad_add_fusion), channel_id=1, source_target_pairs={{0,8},{4,12},{8,0},{12,4},{1,9},{5,13},{9,1},{13,5},{2,10},{6,14},... | collective-permute-start | bytes 11528 | tf_op jit(solution)/shard_map/ppermute | solution.py:346
  9.0 84.4 %collective-permute-start = (s32[3,320]{1,0:T(4,128)S(1)}, s32[3,320]{1,0:T(4,128)S(1)}, u32[]{:S(2)}, u32[]{:S(2)}) collective-permute-start(s32[3,320]{1,0:T(4,128)S(1)} %pad_add_fusion), channel_id=1, source_target_pairs={{0,12},{4,0},{8,4},{12,8},{1,13},{5,1},{9,5},{13,9},{2,14},{6,2},{... | collective-permute-start | bytes 11528 | tf_op jit(solution)/shard_map/ppermute | solution.py:346
  111.5 155.9 %reduce-scatter.2.cloned.1.call-start = ((), (), s32[]{:S(2)}) async-start(), calls=%async_computation.2 | async-start | bytes 15728640 | tf_op jit(solution)/shard_map/reduce_scatter | solution.py:373
  153.1 0.9 copy-start.2
  167.5 99.8 %copy-start = (f32[288,2048]{1,0:T(8,128)S(1)}, f32[288,2048]{1,0:T(8,128)}, u32[]{:S(2)}) copy-start(f32[288,2048]{1,0:T(8,128)} %shard_map.73.first_ref) | copy-start | bytes 7077892
  167.6 99.8 %copy-start.1 = (f32[128,2048]{1,0:T(8,128)S(1)}, f32[128,2048]{1,0:T(8,128)}, u32[]{:S(2)}) copy-start(f32[128,2048]{1,0:T(8,128)} %shard_map.75.second_ref) | copy-start | bytes 3145732
Sparse Core Ops, SparseCore 0:
  8.9 83.1 all-gather.2
  111.6 34.5 all-reduce.1
  167.7 99.6 reduce-scatter.1

commit v5 on v4

--- a/solution.py
+++ b/solution.py
@@ -1,5 +1,4 @@
 import functools
-import math
 
 import jax
 import jax.numpy as jnp
@@ -280,38 +279,32 @@
     )(wanted, operand, slots, maps)
 
 
-def mix_kernel(ends, residual_ref, lora_ref, first_ref, second_ref, third_ref, out_ref):
-    i = pl.program_id(0)
-
-    def mix(projected_ref):
-        out_ref[...] = (
-            residual_ref[...].astype(jnp.float32)
-            + projected_ref[...]
-            + adapter_scale * lora_ref[...].astype(jnp.float32)
+def mix_kernel(residual_ref, lora_ref, *refs):
+    pieces, out_ref = refs[:-1], refs[-1]
+    start = 0
+    for piece in pieces:
+        here = pl.ds(start, piece.shape[0])
+        out_ref[here] = (
+            residual_ref[here].astype(jnp.float32)
+            + piece[...]
+            + adapter_scale * lora_ref[here].astype(jnp.float32)
         ).astype(jnp.bfloat16)
-
-    pl.when(i < ends[0])(lambda: mix(first_ref))
-    pl.when((i >= ends[0]) & (i < ends[1]))(lambda: mix(second_ref))
-    pl.when(i >= ends[1])(lambda: mix(third_ref))
+        start += piece.shape[0]
 
 
 def mix(residual, lora, *pieces):
     rows, width = residual.shape
-    size = math.gcd(*(piece.shape[0] for piece in pieces))
-    block = (size, width)
-    counts = [piece.shape[0] // size for piece in pieces]
-    starts = [0, counts[0], counts[0] + counts[1]]
-
-    def of_piece(start, count):
-        return pl.BlockSpec(block, lambda i: (jnp.clip(i - start, 0, count - 1), 0))
+    tile = min(256, width)
+
+    def columns(array):
+        return pl.BlockSpec((array.shape[0], tile), lambda i: (0, i))
 
     return pl.pallas_call(
-        functools.partial(mix_kernel, starts[1:]),
+        mix_kernel,
         out_shape=jax.ShapeDtypeStruct((rows, width), jnp.bfloat16),
-        grid=(rows // size,),
-        in_specs=[pl.BlockSpec(block, lambda i: (i, 0))] * 2
-        + [of_piece(start, count) for start, count in zip(starts, counts)],
-        out_specs=pl.BlockSpec(block, lambda i: (i, 0)),
+        grid=(width // tile,),
+        in_specs=[columns(array) for array in (residual, lora, *pieces)],
+        out_specs=columns(residual),
         compiler_params=pltpu.CompilerParams(vmem_limit_bytes=48 * 2**20),
     )(residual, lora, *pieces)
 
@@ -351,7 +344,7 @@
     slots = small[:, :, owners * per_owner :] - me * per_owner
     slots = slots.reshape(batches, row_count, 1)
 
-    ends = rows * 3 // 8 // 32 * 32, rows * 13 // 24 // 32 * 32
+    ends = rows * 3 // 8 // 16 * 16, rows * 25 // 48 // 16 * 16
     flat = attention.reshape(rows, feature_count)
     first = project(flat, output_weight, n, 0, ends[0], 1)
     everyone, first = lax.optimization_barrier((everyone, first))

time: 292 us -> 281 us (0.962)
  Pallas kernels: 267 us -> 259 us
    pallas_call x1, Pallas kernels: 15.2 us -> 7.74 us  [mix(): pl.pallas_call(mix_kernel, out_shape=jax.ShapeDtypeStruct((rows, width),...]
  transfers between devices with their start and end apart: 6 -> 6, of which waited for: 1 -> 0; matrix products, arithmetic and copies ran while one was open for 1% -> 1% of each run, Pallas kernels for 77% -> 79%
where the time goes in v5:
time: 281 us; the launch traced here: 279 us
  Pallas kernels  259 us (92%)
  between operations  13.3 us (5%)
  starting transfers between devices  3.04 us (1%)
    pallas_call x3, Pallas kernels, project(): pl.pallas_call(functools.partial(project_kernel, n, per_block, tile, star...  222 us
    pallas_call x2, Pallas kernels, with_adapters(): pl.pallas_call(kernel, out_shape=jax.ShapeDtypeStruct(out_shape, jnp.bflo...  29.7 us
    pallas_call x1, Pallas kernels, mix(): pl.pallas_call(mix_kernel, out_shape=jax.ShapeDtypeStruct((rows, width),...  7.74 us
  transfers between devices with their start and end apart: 6, of which 0 were waited for; matrix products, arithmetic and copies ran while one was open for 1% of the time, Pallas kernels for 79%

profile of v5, /device:TPU:16, one launch (start us, length us, event | category | flops | bytes accessed | tf_op | source)
XLA Modules:
  0.0 279.4 jit_solution(10824309014554686213)
XLA Ops:
  6.5 0.7 all-gather.3.cloned.1.call-update
  7.3 0.0 all-reduce.2.cloned.1.call-start
  7.3 0.1 reshape_squeeze.3
  7.4 0.1 pad_add_fusion
  7.5 1.6 collective-permute-start.1
  9.0 1.4 collective-permute-start
  10.4 83.0 %shard_map.73.refs_0_ = f32[288,2048]{1,0:T(8,128)} custom-call(bf16[768,2048]{1,0:T(8,128)(2,1)} %bitcast.13, bf16[2048,8192]{1,0:T(8,128)(2,1)} %w_hbm.5), custom_call_target="tpu_custom_call" | custom-call | flops 9663676416 | bytes 71303168 | tf_op jit(solution)/shard_map/pallas_call | solution.py:168
  93.4 0.0 collective-permute-done.2
  93.4 0.1 select_select_fusion
  93.6 0.1 reshape.46
  93.7 0.1 slice_subtract_fusion
  93.7 1.5 reshape.53.slots_ref
  95.2 0.0 all-gather.3.cloned.1.call-done
  95.2 16.2 %shard_map.74 = bf16[12,16,256]{2,1,0:T(8,128)(2,1)} custom-call(s32[12,16]{1,0:T(8,128)S(1)} %bitcast.10, bf16[12,256,2048]{2,1,0:T(8,128)(2,1)} %all-gather.3.cloned.1.call-done, s32[12,256,1]{2,1,0:T(8,128)S(1)} %reshape.53.slots_ref, bf16[256,16,2048]{2,1,0:T(8,128)(2,1)} %maps_hbm.2), custom_call_target="tpu_custom_call" | custom-call | tf_op jit(solution)/shard_map/pallas_call | solution.py:263
  111.5 0.0 all-reduce.2.cloned.1.call-update
  111.5 0.0 reduce-scatter.2.cloned.1.call-start
  111.5 37.4 %shard_map.75.refs_1_ = f32[112,2048]{1,0:T(8,128)} custom-call(bf16[768,2048]{1,0:T(8,128)(2,1)} %bitcast.14, bf16[2048,8192]{1,0:T(8,128)(2,1)} %w_hbm.5), custom_call_target="tpu_custom_call" | custom-call | flops 3758096384 | bytes 48234496 | tf_op jit(solution)/shard_map/pallas_call | solution.py:168
  148.9 0.0 all-reduce.2.cloned.1.call-done.shrink_ref
  149.0 0.9 copy-done.2
  149.9 13.4 %shard_map.76 = bf16[12,256,2048]{2,1,0:T(8,128)(2,1)} custom-call(s32[12,16]{1,0:T(8,128)S(1)} %bitcast.11, bf16[12,16,256]{2,1,0:T(8,128)(2,1)S(1)} %copy-done.2, s32[12,256,1]{2,1,0:T(8,128)S(1)} %reshape.53.slots_ref, bf16[256,16,2048]{2,1,0:T(8,128)(2,1)} %maps_hbm.3), custom_call_target="tpu_custom_call" | custom-call | tf_op jit(solution)/shard_map/pallas_call | solution.py:263
  163.3 0.0 reduce-scatter.2.cloned.1.call-update
  163.3 101.7 %shard_map.77.refs_2_ = f32[368,2048]{1,0:T(8,128)} custom-call(bf16[768,2048]{1,0:T(8,128)(2,1)} %bitcast.15, bf16[2048,8192]{1,0:T(8,128)(2,1)} %w_hbm.5), custom_call_target="tpu_custom_call" | custom-call | flops 12348030976 | bytes 81788928 | tf_op jit(solution)/shard_map/pallas_call | solution.py:168
  265.0 0.0 reduce-scatter.2.cloned.1.call-done
  265.1 7.7 %shard_map.78 = bf16[768,2048]{1,0:T(8,128)(2,1)} custom-call(bf16[768,2048]{1,0:T(8,128)(2,1)} %bitcast.16, bf16[768,2048]{1,0:T(8,128)(2,1)} %bitcast.17, f32[288,2048]{1,0:T(8,128)S(1)} %copy-done, f32[112,2048]{1,0:T(8,128)S(1)} %copy-done.1, f32[368,2048]{1,0:T(8,128)} %shard_map.77.refs_2_), custom_call_target="tpu_custom_call" | custom-call | tf_op jit(solution)/shard_map/pallas_call | solution.py:302
  (18 shorter events, 0.1 us)
Async XLA Ops:
  6.5 0.8 copy-start.3
  6.5 0.9 copy-start.4
  6.5 88.7 %all-gather.3.cloned.1.call-start = ((), (), s32[]{:S(2)}) async-start(), calls=%async_computation.3 | async-start | bytes 15728640 | tf_op jit(solution)/shard_map/all_gather | solution.py:331
  7.3 141.7 %all-reduce.2.cloned.1.call-start = ((), (), s32[]{:S(2)}) async-start(), calls=%async_computation.1 | async-start | bytes 196608 | tf_op jit(solution)/shard_map/psum | solution.py:358
  7.5 85.9 %collective-permute-start.2 = (s32[3,320]{1,0:T(4,128)S(1)}, s32[3,320]{1,0:T(4,128)S(1)}, u32[]{:S(2)}, u32[]{:S(2)}) collective-permute-start(s32[3,320]{1,0:T(4,128)S(1)} %pad_add_fusion), channel_id=1, source_target_pairs={{0,4},{4,8},{8,12},{12,0},{1,5},{5,9},{9,13},{13,1},{2,6},{6,10},{... | collective-permute-start | bytes 11528 | tf_op jit(solution)/shard_map/ppermute | solution.py:339
  7.5 85.9 %collective-permute-start.1 = (s32[3,320]{1,0:T(4,128)S(1)}, s32[3,320]{1,0:T(4,128)S(1)}, u32[]{:S(2)}, u32[]{:S(2)}) collective-permute-start(s32[3,320]{1,0:T(4,128)S(1)} %pad_add_fusion), channel_id=1, source_target_pairs={{0,8},{4,12},{8,0},{12,4},{1,9},{5,13},{9,1},{13,5},{2,10},{6,14},... | collective-permute-start | bytes 11528 | tf_op jit(solution)/shard_map/ppermute | solution.py:339
  9.0 84.4 %collective-permute-start = (s32[3,320]{1,0:T(4,128)S(1)}, s32[3,320]{1,0:T(4,128)S(1)}, u32[]{:S(2)}, u32[]{:S(2)}) collective-permute-start(s32[3,320]{1,0:T(4,128)S(1)} %pad_add_fusion), channel_id=1, source_target_pairs={{0,12},{4,0},{8,4},{12,8},{1,13},{5,1},{9,5},{13,9},{2,14},{6,2},{... | collective-permute-start | bytes 11528 | tf_op jit(solution)/shard_map/ppermute | solution.py:339
  111.5 153.6 %reduce-scatter.2.cloned.1.call-start = ((), (), s32[]{:S(2)}) async-start(), calls=%async_computation.2 | async-start | bytes 15728640 | tf_op jit(solution)/shard_map/reduce_scatter | solution.py:366
  149.0 0.9 copy-start.2
  163.3 101.7 %copy-start = (f32[288,2048]{1,0:T(8,128)S(1)}, f32[288,2048]{1,0:T(8,128)}, u32[]{:S(2)}) copy-start(f32[288,2048]{1,0:T(8,128)} %shard_map.73.refs_0_) | copy-start | bytes 7077892
  163.3 101.7 %copy-start.1 = (f32[112,2048]{1,0:T(8,128)S(1)}, f32[112,2048]{1,0:T(8,128)}, u32[]{:S(2)}) copy-start(f32[112,2048]{1,0:T(8,128)} %shard_map.75.refs_1_) | copy-start | bytes 2752516
Sparse Core Ops, SparseCore 0:
  8.9 83.1 all-gather.2
  111.6 34.2 all-reduce.1
  163.4 99.7 reduce-scatter.1
